TPU v7x, 32 devices: a whole 2x2x4 slice. The times are simulated.
32 devices in a mesh: section: 4 (over y, x), dp: 8 (over z, core).
Axes of the slice: x: 2, y: 2, z: 4, core: 2. Of those that a mesh axis runs over, the one named last changes fastest.
Arguments:
- stream_in: bfloat16 [2, 512, 3584], P(None, 'dp'), may hold values from -6 to 6
- cotangent: bfloat16 [2, 512, 3584], P(None, 'dp'), may hold values from -6 to 6
- norm_gain: bfloat16 [4, 3584], P('section'), may hold values from 0.1 to 3.5
- weight_in: bfloat16 [4, 3584, 128], P('section', 'dp'), may hold values from -0.09375 to 0.09375
- weight_out: bfloat16 [4, 128, 3584], P('section', 'dp'), may hold values from -0.5 to 0.5
- moment_in: float32 [4, 3584, 128], P('section', 'dp'), may hold values from -3 to 3
- variance_in: float32 [4, 3584, 128], P('section', 'dp'), may hold values from 0.05 to 2
- moment_out: float32 [4, 128, 3584], P('section', 'dp'), may hold values from -3 to 3
- variance_out: float32 [4, 128, 3584], P('section', 'dp'), may hold values from 0.05 to 2
Outputs:
- weight_in_next: float32 [4, 3584, 128], P('section', 'dp')
- moment_in_next: float32 [4, 3584, 128], P('section', 'dp')
- variance_in_next: float32 [4, 3584, 128], P('section', 'dp')
- weight_out_next: float32 [4, 128, 3584], P('section', 'dp')
- moment_out_next: float32 [4, 128, 3584], P('section', 'dp')
- variance_out_next: float32 [4, 128, 3584], P('section', 'dp')
All inputs are finite; a program needn't handle non-finite values.
Results may differ from a plain program's by a relative error of at most 0.02.
Values may be sent and summed in bfloat16 or wider, within the bound.
A program may use at most 64 MiB of HBM per device.

v0:
```python
import jax
import jax.numpy as jnp
from jax import lax
from jax.sharding import PartitionSpec as P

E = 3584
R = 128


NORM_EPS = 1e-06
BETA_ONE = 0.9
BETA_TWO = 0.95
STEP_RATE = 0.01
ADAM_EPS = 1e-08
CLIP_EPS = 1e-06


def from_behind(x, axis, by):
    count = lax.axis_size(axis)
    pairs = [(i, i + by) for i in range(count) if 0 <= i + by < count]
    return lax.ppermute(x, axis, pairs)


def normalize(stream, gain):
    values = stream.astype(jnp.float32)
    inv_root = lax.rsqrt(jnp.mean(values * values, axis=-1, keepdims=True) + NORM_EPS)
    unit_rows = values * inv_root
    normed = (unit_rows * gain.astype(jnp.float32)).astype(jnp.bfloat16)
    return (values, inv_root, unit_rows, normed)


def section_forward(stream, gain, in_weight, out_weight):
    values, inv_root, unit_rows, normed = normalize(stream, gain)
    pre_act = jnp.dot(normed, in_weight, preferred_element_type=jnp.float32)
    hidden = (pre_act * jax.nn.sigmoid(pre_act)).astype(jnp.bfloat16)
    return (values + jnp.dot(hidden, out_weight, preferred_element_type=jnp.float32)).astype(
        jnp.bfloat16
    )


def section_backward(stream, grad_rows, gain, in_weight, out_weight):
    values, inv_root, unit_rows, normed = normalize(stream, gain)
    pre_act = jnp.dot(normed, in_weight, preferred_element_type=jnp.float32)
    squash = jax.nn.sigmoid(pre_act)
    hidden = (pre_act * squash).astype(jnp.bfloat16)
    grad_hidden = lax.dot_general(
        grad_rows, out_weight, (((1,), (1,)), ((), ())), preferred_element_type=jnp.float32
    )
    grad_act = (grad_hidden * squash * (1.0 + pre_act * (1.0 - squash))).astype(jnp.bfloat16)
    grad_normed = lax.dot_general(
        grad_act, in_weight, (((1,), (1,)), ((), ())), preferred_element_type=jnp.float32
    ) * gain.astype(jnp.float32)
    inner_mean = jnp.mean(grad_normed * unit_rows, axis=-1, keepdims=True)
    grad_in = (
        grad_rows.astype(jnp.float32) + inv_root * (grad_normed - unit_rows * inner_mean)
    ).astype(jnp.bfloat16)
    return (grad_in, normed, grad_act, hidden)


def contract_rows(left, right):
    return lax.dot_general(
        left, right, (((0,), (0,)), ((), ())), preferred_element_type=jnp.float32
    )


def forward_tick(step_tick, position, is_first, incoming, saved_rows, inputs, weights):
    batch_count = inputs.shape[0]
    chain_index = step_tick - position
    active = jnp.logical_and(chain_index >= 0, chain_index < batch_count)
    batch_slot = jnp.clip(chain_index, 0, batch_count - 1)
    stream = jnp.where(is_first, lax.dynamic_index_in_dim(inputs, batch_slot, 0, False), incoming)
    kept_row = jnp.where(active, stream, lax.dynamic_index_in_dim(saved_rows, batch_slot, 0, False))
    saved_rows = lax.dynamic_update_index_in_dim(saved_rows, kept_row, batch_slot, 0)
    section_out = lax.cond(
        active, lambda rows_in: section_forward(rows_in, *weights), jnp.zeros_like, stream
    )
    return (section_out, saved_rows)


def backward_tick(
    step_tick, position, is_last, incoming, saved_rows, targets, weights, grad_sums, groups
):
    batch_count = targets.shape[0]
    chain_index = step_tick - position
    active = jnp.logical_and(chain_index >= 0, chain_index < batch_count)
    batch_slot = jnp.clip(chain_index, 0, batch_count - 1)
    grad_rows = jnp.where(
        is_last, lax.dynamic_index_in_dim(targets, batch_slot, 0, False), incoming
    )
    stream = lax.dynamic_index_in_dim(saved_rows, batch_slot, 0, False)
    half_group = batch_slot * groups // batch_count

    def run_section(operands):
        rows_in, grad_now, sums_now = operands
        grad_in, normed, grad_act, hidden = section_backward(rows_in, grad_now, *weights)
        sum_in, sum_out = sums_now
        sum_in = lax.dynamic_update_index_in_dim(
            sum_in,
            lax.dynamic_index_in_dim(sum_in, half_group, 0, False)
            + contract_rows(normed, grad_act),
            half_group,
            0,
        )
        sum_out = lax.dynamic_update_index_in_dim(
            sum_out,
            lax.dynamic_index_in_dim(sum_out, half_group, 0, False)
            + contract_rows(hidden, grad_now),
            half_group,
            0,
        )
        return (grad_in, (sum_in, sum_out))

    def skip_section(operands):
        return (jnp.zeros_like(operands[1]), operands[2])

    return lax.cond(active, run_section, skip_section, (stream, grad_rows, grad_sums))


def update(weight, grad, moment, variance, factor):
    scaled = factor * grad
    moment = BETA_ONE * moment + (1.0 - BETA_ONE) * scaled
    variance = BETA_TWO * variance + (1.0 - BETA_TWO) * scaled * scaled
    weight = weight.astype(jnp.float32) - STEP_RATE * moment / (jnp.sqrt(variance) + ADAM_EPS)
    return (weight[None], moment[None], variance[None])


def shards(
    stream_in,
    cotangent,
    norm_gain,
    weight_in,
    weight_out,
    moment_in,
    variance_in,
    moment_out,
    variance_out,
):
    section_count = lax.axis_size("section")
    section_place = lax.axis_index("section")
    micro_count = stream_in.shape[0]
    in_slice = weight_in[0]
    out_slice = weight_out[0]
    full_in_shape = (in_slice.shape[0] * lax.axis_size("dp"), in_slice.shape[1])
    full_out_shape = (out_slice.shape[0] * lax.axis_size("dp"), out_slice.shape[1])
    empty_stream = jnp.zeros(stream_in.shape[1:], jnp.bfloat16)
    is_first = section_place == 0
    is_last = section_place == section_count - 1
    whole_in, whole_out = (
        lax.all_gather(in_slice, "dp", axis=0, tiled=True),
        lax.all_gather(out_slice, "dp", axis=0, tiled=True),
    )
    own_layer = (norm_gain[0], whole_in, whole_out)
    tick_count = micro_count + section_count - 1

    def run_forward(step_tick, loop_state):
        incoming, saved_rows = loop_state
        section_out, saved_rows = forward_tick(
            step_tick, section_place, is_first, incoming, saved_rows, stream_in, own_layer
        )
        return (from_behind(section_out, "section", 1), saved_rows)

    _, saved_rows = lax.fori_loop(
        0, tick_count, run_forward, (empty_stream, jnp.zeros_like(stream_in))
    )
    start_sums = (
        jnp.zeros((2,) + full_in_shape, jnp.float32),
        jnp.zeros((2,) + full_out_shape, jnp.float32),
    )

    def run_backward(step_tick, loop_state):
        incoming, grad_sums = loop_state
        grad_in, grad_sums = backward_tick(
            step_tick,
            section_count - 1 - section_place,
            is_last,
            incoming,
            saved_rows,
            cotangent,
            own_layer,
            grad_sums,
            2,
        )
        return (from_behind(grad_in, "section", -1), grad_sums)

    _, (stacked_in, stacked_out) = lax.fori_loop(
        0, tick_count, run_backward, (empty_stream, start_sums)
    )
    reduced_in, reduced_out = (
        lax.psum_scatter(
            stacked_in.astype(jnp.bfloat16), "dp", scatter_dimension=1, tiled=True
        ).astype(jnp.float32),
        lax.psum_scatter(
            stacked_out.astype(jnp.bfloat16), "dp", scatter_dimension=1, tiled=True
        ).astype(jnp.float32),
    )
    grad_w_in = reduced_in[0] + reduced_in[1]
    grad_w_out = reduced_out[0] + reduced_out[1]
    local_sum = jnp.sum(grad_w_in * grad_w_in) + jnp.sum(grad_w_out * grad_w_out)
    norm_total = lax.psum(local_sum, ("section", "dp"))
    count_all = 2.0 * E * R * section_count
    factor = jnp.minimum(1.0, lax.rsqrt(norm_total / count_all + CLIP_EPS))
    new_in, new_moment_in, new_variance_in = update(
        in_slice, grad_w_in, moment_in[0], variance_in[0], factor
    )
    new_out, new_moment_out, new_variance_out = update(
        out_slice, grad_w_out, moment_out[0], variance_out[0], factor
    )
    return (new_in, new_moment_in, new_variance_in, new_out, new_moment_out, new_variance_out)


def solution(mesh):
    return jax.shard_map(
        shards,
        mesh=mesh,
        in_specs=(
            P(None, "dp", None),
            P(None, "dp", None),
            P("section", None),
            P("section", "dp", None),
            P("section", "dp", None),
            P("section", "dp", None),
            P("section", "dp", None),
            P("section", "dp", None),
            P("section", "dp", None),
        ),
        out_specs=(
            P("section", "dp", None),
            P("section", "dp", None),
            P("section", "dp", None),
            P("section", "dp", None),
            P("section", "dp", None),
            P("section", "dp", None),
        ),
        check_vma=False,
    )
```

profile of v0, /device:TPU:0, one launch (start us, length us, event | category | flops | bytes accessed | tf_op | source)
XLA Modules:
  0.0 356.6 jit_solution(14173309962649610052)
XLA Ops:
  7.2 17.8 %all-gather = bf16[1,3584,128]{2,1,0:T(8,128)(2,1)S(1)} all-gather(bf16[1,448,128]{2,1,0:T(8,128)(2,1)} %param.20), channel_id=2, replica_groups=mesh['section'=4,'dp'=8] {'dp'}, dimensions={1}, use_global_device_ids=true | all-gather | bytes 1032192 | tf_op jit(solution)/shard_map/all_gather | solution.py:149
  25.1 16.8 %all-gather.1 = bf16[1,128,3584]{2,1,0:T(8,128)(2,1)S(1)} all-gather(bf16[1,16,3584]{2,1,0:T(8,128)(2,1)} %param.21), channel_id=3, replica_groups=mesh['section'=4,'dp'=8] {'dp'}, dimensions={1}, use_global_device_ids=true | all-gather | bytes 1032192 | tf_op jit(solution)/shard_map/all_gather | solution.py:150
  42.6 0.8 broadcast.93.clone
  43.5 83.1 %while.34 = (s32[]{:T(128)}, bf16[64,3584]{1,0:T(8,128)(2,1)}, bf16[2,64,3584]{2,1,0:T(8,128)(2,1)S(1)}, s32[]{:T(128)}, pred[]{:T(512)}, /*index=5*/bf16[2,64,3...) while((s32[]{:T(128)}, bf16[64,3584]{1,0:T(8,128)(2,1)}, ...), condition=%wide.region_4.5_spmd, body=%wide.region_0.4_spmd.sunk | while | flops 120237640 | bytes 10129705 | solution.py:162
  43.6 1.2 bitcast_dynamic-update-slice_fusion.2
  44.8 1.6 conditional.4
  45.1 1.4 fusion
  46.4 2.8 collective-permute-start
  49.2 10.6 %collective-permute-done = bf16[64,3584]{1,0:T(8,128)(2,1)S(1)} collective-permute-done((bf16[64,3584]{1,0:T(8,128)(2,1)}, bf16[64,3584]{1,0:T(8,128)(2,1)S(1)}, u32[]{:S(2)}, u32[]{:S(2)}) %collective-permute-start) | collective-permute-done | bytes 458784 | tf_op jit(solution)/shard_map/while/body/eval_jaxpr/ppermute | solution.py:21
  60.6 1.2 bitcast_dynamic-update-slice_fusion.2
  61.8 1.6 conditional.4
  62.0 1.4 fusion
  63.4 4.4 %collective-permute-start = (bf16[64,3584]{1,0:T(8,128)(2,1)}, bf16[64,3584]{1,0:T(8,128)(2,1)S(1)}, u32[]{:S(2)}, u32[]{:S(2)}) collective-permute-start(bf16[64,3584]{1,0:T(8,128)(2,1)} %get-tuple-element.931), channel_id=1, source_target_pairs={{0,8},{8,16},{16,24},{1,9},{9,17},{17,25},{2,10},{10,18},{18,26},{... | collective-permute-start | bytes 1376264 | tf_op jit(solution)/shard_map/while/body/eval_jaxpr/ppermute | solution.py:21
  67.8 9.7 %collective-permute-done = bf16[64,3584]{1,0:T(8,128)(2,1)S(1)} collective-permute-done((bf16[64,3584]{1,0:T(8,128)(2,1)}, bf16[64,3584]{1,0:T(8,128)(2,1)S(1)}, u32[]{:S(2)}, u32[]{:S(2)}) %collective-permute-start) | collective-permute-done | bytes 458784 | tf_op jit(solution)/shard_map/while/body/eval_jaxpr/ppermute | solution.py:21
  78.4 1.2 bitcast_dynamic-update-slice_fusion.2
  79.6 0.8 conditional.4
  79.6 0.8 broadcast.84
  80.4 5.2 %collective-permute-start = (bf16[64,3584]{1,0:T(8,128)(2,1)}, bf16[64,3584]{1,0:T(8,128)(2,1)S(1)}, u32[]{:S(2)}, u32[]{:S(2)}) collective-permute-start(bf16[64,3584]{1,0:T(8,128)(2,1)} %get-tuple-element.931), channel_id=1, source_target_pairs={{0,8},{8,16},{16,24},{1,9},{9,17},{17,25},{2,10},{10,18},{18,26},{... | collective-permute-start | bytes 1376264 | tf_op jit(solution)/shard_map/while/body/eval_jaxpr/ppermute | solution.py:21
  85.7 8.8 %collective-permute-done = bf16[64,3584]{1,0:T(8,128)(2,1)S(1)} collective-permute-done((bf16[64,3584]{1,0:T(8,128)(2,1)}, bf16[64,3584]{1,0:T(8,128)(2,1)S(1)}, u32[]{:S(2)}, u32[]{:S(2)}) %collective-permute-start) | collective-permute-done | bytes 458784 | tf_op jit(solution)/shard_map/while/body/eval_jaxpr/ppermute | solution.py:21
  95.3 1.2 bitcast_dynamic-update-slice_fusion.2
  96.5 0.8 conditional.4
  96.5 0.8 broadcast.84
  97.3 4.6 %collective-permute-start = (bf16[64,3584]{1,0:T(8,128)(2,1)}, bf16[64,3584]{1,0:T(8,128)(2,1)S(1)}, u32[]{:S(2)}, u32[]{:S(2)}) collective-permute-start(bf16[64,3584]{1,0:T(8,128)(2,1)} %get-tuple-element.931), channel_id=1, source_target_pairs={{0,8},{8,16},{16,24},{1,9},{9,17},{17,25},{2,10},{10,18},{18,26},{... | collective-permute-start | bytes 1376264 | tf_op jit(solution)/shard_map/while/body/eval_jaxpr/ppermute | solution.py:21
  101.9 7.9 %collective-permute-done = bf16[64,3584]{1,0:T(8,128)(2,1)S(1)} collective-permute-done((bf16[64,3584]{1,0:T(8,128)(2,1)}, bf16[64,3584]{1,0:T(8,128)(2,1)S(1)}, u32[]{:S(2)}, u32[]{:S(2)}) %collective-permute-start) | collective-permute-done | bytes 458784 | tf_op jit(solution)/shard_map/while/body/eval_jaxpr/ppermute | solution.py:21
  110.7 1.2 bitcast_dynamic-update-slice_fusion.2
  111.9 0.8 conditional.4
  111.9 0.8 broadcast.84
  112.7 6.1 %collective-permute-start = (bf16[64,3584]{1,0:T(8,128)(2,1)}, bf16[64,3584]{1,0:T(8,128)(2,1)S(1)}, u32[]{:S(2)}, u32[]{:S(2)}) collective-permute-start(bf16[64,3584]{1,0:T(8,128)(2,1)} %get-tuple-element.931), channel_id=1, source_target_pairs={{0,8},{8,16},{16,24},{1,9},{9,17},{17,25},{2,10},{10,18},{18,26},{... | collective-permute-start | bytes 1376264 | tf_op jit(solution)/shard_map/while/body/eval_jaxpr/ppermute | solution.py:21
  118.8 7.0 %collective-permute-done = bf16[64,3584]{1,0:T(8,128)(2,1)S(1)} collective-permute-done((bf16[64,3584]{1,0:T(8,128)(2,1)}, bf16[64,3584]{1,0:T(8,128)(2,1)S(1)}, u32[]{:S(2)}, u32[]{:S(2)}) %collective-permute-start) | collective-permute-done | bytes 458784 | tf_op jit(solution)/shard_map/while/body/eval_jaxpr/ppermute | solution.py:21
  126.6 2.3 broadcast_in_dim.44
  128.9 2.0 broadcast_in_dim.43
  130.9 101.1 %while.35 = (s32[]{:T(128)}, bf16[64,3584]{1,0:T(8,128)(2,1)S(1)}, f32[2,3584,128]{2,1,0:T(8,128)}, f32[2,128,3584]{2,1,0:T(8,128)}, s32[]{:T(128)}, /*index=5*/...) while((s32[]{:T(128)}, bf16[64,3584]{1,0:T(8,128)(2,1)S(1)}, ...), condition=%wide.region_10.11_spmd, body=%wide.region_5.10_spmd.sunk | while | flops 300371520 | bytes 85547984 | solution.py:185
  131.7 1.3 collective-permute-start.1
  133.0 10.6 %collective-permute-done.1 = bf16[64,3584]{1,0:T(8,128)(2,1)S(1)} collective-permute-done((bf16[64,3584]{1,0:T(8,128)(2,1)}, bf16[64,3584]{1,0:T(8,128)(2,1)S(1)}, u32[]{:S(2)}, u32[]{:S(2)}) %collective-permute-start.1) | collective-permute-done | bytes 458784 | tf_op jit(solution)/shard_map/while/body/eval_jaxpr/ppermute | solution.py:21
  144.4 1.3 collective-permute-start.1
  145.7 10.5 %collective-permute-done.1 = bf16[64,3584]{1,0:T(8,128)(2,1)S(1)} collective-permute-done((bf16[64,3584]{1,0:T(8,128)(2,1)}, bf16[64,3584]{1,0:T(8,128)(2,1)S(1)}, u32[]{:S(2)}, u32[]{:S(2)}) %collective-permute-start.1) | collective-permute-done | bytes 458784 | tf_op jit(solution)/shard_map/while/body/eval_jaxpr/ppermute | solution.py:21
  156.3 0.8 conditional.5
  157.1 1.3 collective-permute-start.1
  158.4 32.6 %collective-permute-done.1 = bf16[64,3584]{1,0:T(8,128)(2,1)S(1)} collective-permute-done((bf16[64,3584]{1,0:T(8,128)(2,1)}, bf16[64,3584]{1,0:T(8,128)(2,1)S(1)}, u32[]{:S(2)}, u32[]{:S(2)}) %collective-permute-start.1) | collective-permute-done | bytes 458784 | tf_op jit(solution)/shard_map/while/body/eval_jaxpr/ppermute | solution.py:21
  191.0 9.5 %conditional.5 = (bf16[64,3584]{1,0:T(8,128)(2,1)}, f32[2,3584,128]{2,1,0:T(8,128)}, f32[2,128,3584]{2,1,0:T(8,128)}) conditional(s32[]{:T(128)} %convert_element_type.142, (f32[2,3584,128]{2,1,0:T(8,128)}, f32[2,128,3584]{2,1,0:T(8,128)}) %tuple.102, (pred[]{:T(512)}, bf16[2,64,3584]{2,1,0:T(8,128)(2,1)}, s32[]{:T(128)}, ...), branch_computations={%region_6.6_spmd, %region_7.9_spmd} | conditional | flops 300371520 | bytes 83712624 | solution.py:116
  191.5 1.2 bitcast_select_fusion.2
  193.7 1.1 fusion.28
  195.5 1.4 copy-done
  197.4 1.2 copy-done.3
  198.6 1.8 copy-done.1
  200.5 1.3 collective-permute-start.1
  201.7 10.2 %collective-permute-done.1 = bf16[64,3584]{1,0:T(8,128)(2,1)S(1)} collective-permute-done((bf16[64,3584]{1,0:T(8,128)(2,1)}, bf16[64,3584]{1,0:T(8,128)(2,1)S(1)}, u32[]{:S(2)}, u32[]{:S(2)}) %collective-permute-start.1) | collective-permute-done | bytes 458784 | tf_op jit(solution)/shard_map/while/body/eval_jaxpr/ppermute | solution.py:21
  211.9 9.5 %conditional.5 = (bf16[64,3584]{1,0:T(8,128)(2,1)}, f32[2,3584,128]{2,1,0:T(8,128)}, f32[2,128,3584]{2,1,0:T(8,128)}) conditional(s32[]{:T(128)} %convert_element_type.142, (f32[2,3584,128]{2,1,0:T(8,128)}, f32[2,128,3584]{2,1,0:T(8,128)}) %tuple.102, (pred[]{:T(512)}, bf16[2,64,3584]{2,1,0:T(8,128)(2,1)}, s32[]{:T(128)}, ...), branch_computations={%region_6.6_spmd, %region_7.9_spmd} | conditional | flops 300371520 | bytes 83712624 | solution.py:116
  212.5 1.2 bitcast_select_fusion.2
  214.7 1.1 fusion.28
  216.4 1.4 copy-done
  218.4 1.2 copy-done.3
  219.6 1.8 copy-done.1
  221.4 1.3 collective-permute-start.1
  222.7 9.3 %collective-permute-done.1 = bf16[64,3584]{1,0:T(8,128)(2,1)S(1)} collective-permute-done((bf16[64,3584]{1,0:T(8,128)(2,1)}, bf16[64,3584]{1,0:T(8,128)(2,1)S(1)}, u32[]{:S(2)}, u32[]{:S(2)}) %collective-permute-start.1) | collective-permute-done | bytes 458784 | tf_op jit(solution)/shard_map/while/body/eval_jaxpr/ppermute | solution.py:21
  232.0 3.6 %convert_element_type.99 = bf16[2,3584,128]{2,1,0:T(8,128)(2,1)} convert(f32[2,3584,128]{2,1,0:T(8,128)} %get-tuple-element.659) | non-fusion elementwise | flops 917504 | bytes 5505024 | tf_op jit(solution)/shard_map/convert_element_type | solution.py:190
  235.7 3.5 convert_element_type.101
  239.3 31.3 %reduce-scatter.3.cloned.1.call-done = bf16[2,448,128]{2,1,0:T(8,128)(2,1)} async-done(((bf16[2,3584,128]{2,1,0:T(8,128)(2,1)}), bf16[2,448,128]{2,1,0:T(8,128)(2,1)}) %reduce-scatter.3.cloned.1.call-update) | async-done | bytes 229392 | tf_op jit(solution)/shard_map/reduce_scatter | solution.py:189
  270.6 1.0 convert_element_type.100
  272.2 34.2 %reduce-scatter.5.cloned.1.call-done = bf16[2,16,3584]{2,1,0:T(8,128)(2,1)} async-done(((bf16[2,128,3584]{2,1,0:T(8,128)(2,1)}), bf16[2,16,3584]{2,1,0:T(8,128)(2,1)}) %reduce-scatter.5.cloned.1.call-update) | async-done | bytes 229392 | tf_op jit(solution)/shard_map/reduce_scatter | solution.py:192
  306.4 1.0 convert_element_type.102
  309.3 37.8 %psum.7 = f32[]{:T(128)} all-reduce(f32[]{:T(128)S(6)} %add.185), channel_id=1, replica_groups=mesh['section'=4,'dp'=8] {'section','dp'}, use_global_device_ids=true, to_apply=%region_15.16 | all-reduce | flops 1 | bytes 8 | tf_op jit(solution)/shard_map/psum | solution.py:199
  347.9 0.9 divide_subtract_fusion
  348.8 0.9 divide_subtract_fusion.1
  (79 shorter events, 16.2 us)
Async XLA Ops:
  7.2 263.4 %reduce-scatter.3.cloned.1.call-start = ((), (), s32[]{:S(2)}) async-start(), calls=%async_computation.2 | async-start | bytes 2064384 | tf_op jit(solution)/shard_map/reduce_scatter | solution.py:189
  46.4 13.3 %collective-permute-start = (bf16[64,3584]{1,0:T(8,128)(2,1)}, bf16[64,3584]{1,0:T(8,128)(2,1)S(1)}, u32[]{:S(2)}, u32[]{:S(2)}) collective-permute-start(bf16[64,3584]{1,0:T(8,128)(2,1)} %get-tuple-element.931), channel_id=1, source_target_pairs={{0,8},{8,16},{16,24},{1,9},{9,17},{17,25},{2,10},{10,18},{18,26},{... | collective-permute-start | bytes 1376264 | tf_op jit(solution)/shard_map/while/body/eval_jaxpr/ppermute | solution.py:21
  59.8 0.8 copy-start.4
  63.4 14.2 %collective-permute-start = (bf16[64,3584]{1,0:T(8,128)(2,1)}, bf16[64,3584]{1,0:T(8,128)(2,1)S(1)}, u32[]{:S(2)}, u32[]{:S(2)}) collective-permute-start(bf16[64,3584]{1,0:T(8,128)(2,1)} %get-tuple-element.931), channel_id=1, source_target_pairs={{0,8},{8,16},{16,24},{1,9},{9,17},{17,25},{2,10},{10,18},{18,26},{... | collective-permute-start | bytes 1376264 | tf_op jit(solution)/shard_map/while/body/eval_jaxpr/ppermute | solution.py:21
  77.6 0.8 copy-start.4
  80.4 14.1 %collective-permute-start = (bf16[64,3584]{1,0:T(8,128)(2,1)}, bf16[64,3584]{1,0:T(8,128)(2,1)S(1)}, u32[]{:S(2)}, u32[]{:S(2)}) collective-permute-start(bf16[64,3584]{1,0:T(8,128)(2,1)} %get-tuple-element.931), channel_id=1, source_target_pairs={{0,8},{8,16},{16,24},{1,9},{9,17},{17,25},{2,10},{10,18},{18,26},{... | collective-permute-start | bytes 1376264 | tf_op jit(solution)/shard_map/while/body/eval_jaxpr/ppermute | solution.py:21
  94.5 0.8 copy-start.4
  97.3 12.5 %collective-permute-start = (bf16[64,3584]{1,0:T(8,128)(2,1)}, bf16[64,3584]{1,0:T(8,128)(2,1)S(1)}, u32[]{:S(2)}, u32[]{:S(2)}) collective-permute-start(bf16[64,3584]{1,0:T(8,128)(2,1)} %get-tuple-element.931), channel_id=1, source_target_pairs={{0,8},{8,16},{16,24},{1,9},{9,17},{17,25},{2,10},{10,18},{18,26},{... | collective-permute-start | bytes 1376264 | tf_op jit(solution)/shard_map/while/body/eval_jaxpr/ppermute | solution.py:21
  109.9 0.8 copy-start.4
  112.7 13.1 %collective-permute-start = (bf16[64,3584]{1,0:T(8,128)(2,1)}, bf16[64,3584]{1,0:T(8,128)(2,1)S(1)}, u32[]{:S(2)}, u32[]{:S(2)}) collective-permute-start(bf16[64,3584]{1,0:T(8,128)(2,1)} %get-tuple-element.931), channel_id=1, source_target_pairs={{0,8},{8,16},{16,24},{1,9},{9,17},{17,25},{2,10},{10,18},{18,26},{... | collective-permute-start | bytes 1376264 | tf_op jit(solution)/shard_map/while/body/eval_jaxpr/ppermute | solution.py:21
  125.8 0.8 copy-start.4
  131.7 11.9 %collective-permute-start.1 = (bf16[64,3584]{1,0:T(8,128)(2,1)}, bf16[64,3584]{1,0:T(8,128)(2,1)S(1)}, u32[]{:S(2)}, u32[]{:S(2)}) collective-permute-start(bf16[64,3584]{1,0:T(8,128)(2,1)} %get-tuple-element.844), channel_id=1, source_target_pairs={{8,0},{16,8},{24,16},{9,1},{17,9},{25,17},{10,2},{18,10},{26,18},{... | collective-permute-start | bytes 1376264 | tf_op jit(solution)/shard_map/while/body/eval_jaxpr/ppermute | solution.py:21
  144.4 11.8 %collective-permute-start.1 = (bf16[64,3584]{1,0:T(8,128)(2,1)}, bf16[64,3584]{1,0:T(8,128)(2,1)S(1)}, u32[]{:S(2)}, u32[]{:S(2)}) collective-permute-start(bf16[64,3584]{1,0:T(8,128)(2,1)} %get-tuple-element.844), channel_id=1, source_target_pairs={{8,0},{16,8},{24,16},{9,1},{17,9},{25,17},{10,2},{18,10},{26,18},{... | collective-permute-start | bytes 1376264 | tf_op jit(solution)/shard_map/while/body/eval_jaxpr/ppermute | solution.py:21
  157.1 33.9 %collective-permute-start.1 = (bf16[64,3584]{1,0:T(8,128)(2,1)}, bf16[64,3584]{1,0:T(8,128)(2,1)S(1)}, u32[]{:S(2)}, u32[]{:S(2)}) collective-permute-start(bf16[64,3584]{1,0:T(8,128)(2,1)} %get-tuple-element.844), channel_id=1, source_target_pairs={{8,0},{16,8},{24,16},{9,1},{17,9},{25,17},{10,2},{18,10},{26,18},{... | collective-permute-start | bytes 1376264 | tf_op jit(solution)/shard_map/while/body/eval_jaxpr/ppermute | solution.py:21
  191.5 3.3 copy-start.2
  194.8 2.0 copy-start
  196.8 1.8 copy-start.3
  198.6 1.8 copy-start.1
  200.5 11.5 %collective-permute-start.1 = (bf16[64,3584]{1,0:T(8,128)(2,1)}, bf16[64,3584]{1,0:T(8,128)(2,1)S(1)}, u32[]{:S(2)}, u32[]{:S(2)}) collective-permute-start(bf16[64,3584]{1,0:T(8,128)(2,1)} %get-tuple-element.844), channel_id=1, source_target_pairs={{8,0},{16,8},{24,16},{9,1},{17,9},{25,17},{10,2},{18,10},{26,18},{... | collective-permute-start | bytes 1376264 | tf_op jit(solution)/shard_map/while/body/eval_jaxpr/ppermute | solution.py:21
  212.5 3.3 copy-start.2
  215.8 2.0 copy-start
  217.8 1.8 copy-start.3
  219.6 1.8 copy-start.1
  221.4 10.6 %collective-permute-start.1 = (bf16[64,3584]{1,0:T(8,128)(2,1)}, bf16[64,3584]{1,0:T(8,128)(2,1)S(1)}, u32[]{:S(2)}, u32[]{:S(2)}) collective-permute-start(bf16[64,3584]{1,0:T(8,128)(2,1)} %get-tuple-element.844), channel_id=1, source_target_pairs={{8,0},{16,8},{24,16},{9,1},{17,9},{25,17},{10,2},{18,10},{26,18},{... | collective-permute-start | bytes 1376264 | tf_op jit(solution)/shard_map/while/body/eval_jaxpr/ppermute | solution.py:21
  235.6 70.8 %reduce-scatter.5.cloned.1.call-start = ((), (), s32[]{:S(2)}) async-start(), calls=%async_computation.3 | async-start | bytes 2064384 | tf_op jit(solution)/shard_map/reduce_scatter | solution.py:192
  235.7 112.2 %copy-start.5 = (bf16[1,16,3584]{2,1,0:T(8,128)(2,1)S(1)}, bf16[1,16,3584]{2,1,0:T(8,128)(2,1)}, u32[]{:S(2)}) copy-start(bf16[1,16,3584]{2,1,0:T(8,128)(2,1)} %param.21) | copy-start | bytes 344068
  235.7 112.2 %copy-start.7 = (f32[1,16,3584]{2,1,0:T(8,128)S(1)}, f32[1,16,3584]{2,1,0:T(8,128)}, u32[]{:S(2)}) copy-start(f32[1,16,3584]{2,1,0:T(8,128)} %param.24) | copy-start | bytes 688132
  235.7 112.2 %copy-start.8 = (f32[1,16,3584]{2,1,0:T(8,128)S(1)}, f32[1,16,3584]{2,1,0:T(8,128)}, u32[]{:S(2)}) copy-start(f32[1,16,3584]{2,1,0:T(8,128)} %param.25) | copy-start | bytes 688132
  239.2 109.6 %copy-start.6 = (bf16[1,448,128]{2,1,0:T(8,128)(2,1)S(1)}, bf16[1,448,128]{2,1,0:T(8,128)(2,1)}, u32[]{:S(2)}) copy-start(bf16[1,448,128]{2,1,0:T(8,128)(2,1)} %param.20) | copy-start | bytes 344068
  239.2 109.6 %copy-start.9 = (f32[1,448,128]{2,1,0:T(8,128)S(1)}, f32[1,448,128]{2,1,0:T(8,128)}, u32[]{:S(2)}) copy-start(f32[1,448,128]{2,1,0:T(8,128)} %param.22) | copy-start | bytes 688132
  239.2 109.6 %copy-start.10 = (f32[1,448,128]{2,1,0:T(8,128)S(1)}, f32[1,448,128]{2,1,0:T(8,128)}, u32[]{:S(2)}) copy-start(f32[1,448,128]{2,1,0:T(8,128)} %param.23) | copy-start | bytes 688132
Sparse Core Ops, SparseCore 0:
  235.7 34.8 reduce-scatter.2
  272.9 33.4 reduce-scatter.4
where the time goes:
time: 358 us; the launch traced here: 357 us
  waiting for transfers between devices  183 us (51%)
  blocking collectives  72.5 us (20%)
  starting transfers between devices  29.6 us (8%)
  other arithmetic  24.6 us (7%)
  local copies, waits for them, and re-layouts  23.3 us (7%)
  between operations  16.1 us (4%)
  matrix products  7.27 us (2%)
    ppermute x10, waiting for transfers between devices, from_behind(): return lax.ppermute(x, axis, pairs)  117 us
    psum x1, blocking collectives, shards(): norm_total = lax.psum(local_sum, ('section', 'dp'))  37.8 us
    reduce_scatter x1, waiting for transfers between devices, shards(): lax.psum_scatter(stacked_out.astype(jnp.bfloat16), 'dp', scatter_dimensio...  34.2 us
    reduce_scatter x1, waiting for transfers between devices, shards(): lax.psum_scatter(stacked_in.astype(jnp.bfloat16), 'dp', scatter_dimension...  31.3 us
    ppermute x10, starting transfers between devices, from_behind(): return lax.ppermute(x, axis, pairs)  29.5 us
    all_gather x1, blocking collectives, shards(): lax.all_gather(in_slice, 'dp', axis=0, tiled=True)  17.8 us
    all_gather x1, blocking collectives, shards(): lax.all_gather(out_slice, 'dp', axis=0, tiled=True)  16.8 us
    cond x16, local copies, waits for them, and re-layouts  8.85 us
  transfers between devices with their start and end apart: 12, of which 12 were waited for; matrix products, arithmetic and copies ran while one was open for 1% of the time, Pallas kernels for 0%

commit v1 on v0

--- a/solution.py
+++ b/solution.py
@@ -1,6 +1,10 @@
+import functools
+
 import jax
 import jax.numpy as jnp
 from jax import lax
+from jax.experimental import pallas as pl
+from jax.experimental.pallas import tpu as pltpu
 from jax.sharding import PartitionSpec as P
 
 E = 3584
@@ -208,9 +212,474 @@
     return (new_in, new_moment_in, new_variance_in, new_out, new_moment_out, new_variance_out)
 
 
+MESH = pl.DeviceIdType.MESH
+CORES = 2
+
+
+def dot(left, right, left_dim, right_dim):
+    return lax.dot_general(
+        left, right, (((left_dim,), (right_dim,)), ((), ())), preferred_element_type=jnp.float32
+    )
+
+
+def step_kernel(
+    sections,
+    planes,
+    stream_ref,
+    cotangent_ref,
+    piece_ref,
+    gain_ref,
+    grad_ref,
+    factor_ref,
+    weights,
+    parts,
+    from_core,
+    chip_sums,
+    from_planes,
+    totals,
+    owned,
+    streams,
+    pre_acts,
+    roots,
+    hiddens,
+    sent,
+    received,
+    squares,
+    squares_dp,
+    squares_section,
+    piece_send,
+    piece_recv,
+    rail_send,
+    core_send,
+    weight_recv,
+    swap_send,
+    swap_recv,
+    part_send,
+    part_recv,
+    sum_send,
+    sum_recv,
+    total_send,
+    total_recv,
+    dp_send,
+    dp_recv,
+    section_send,
+    section_recv,
+):
+    me_s = lax.axis_index("section")
+    me_d = lax.axis_index("dp")
+    plane = me_d // CORES
+    core = lax.rem(me_d, CORES)
+    other = 1 - core
+    dp_count = planes * CORES
+    tokens, width = stream_ref.shape
+    channels = width * sections
+    rank = piece_ref.shape[2]
+    tiles = width // 128
+    in_rows = gain_ref.shape[1]
+    out_rows = rank // dp_count
+
+    def section_peer(offset):
+        return (lax.rem(me_s + offset, sections), me_d)
+
+    def dp_peer(offset):
+        return (me_s, lax.rem(me_d + offset, dp_count))
+
+    def plane_peer(offset):
+        return (me_s, lax.rem(plane + offset, planes) * CORES + core)
+
+    partner = (me_s, plane * CORES + other)
+
+    def remote(source, target, send_sem, recv_sem, device):
+        copy = pltpu.make_async_remote_copy(
+            src_ref=source,
+            dst_ref=target,
+            send_sem=send_sem,
+            recv_sem=recv_sem,
+            device_id=device,
+            device_id_type=MESH,
+        )
+        copy.start()
+        started.append(copy)
+        return copy
+
+    def landed(target, sem):
+        pltpu.make_async_copy(target, target, sem).wait()
+
+    started = []
+    barrier = pltpu.get_barrier_semaphore()
+    for offset in range(1, sections):
+        pl.semaphore_signal(barrier, inc=1, device_id=section_peer(offset), device_id_type=MESH)
+    for offset in range(1, dp_count):
+        pl.semaphore_signal(barrier, inc=1, device_id=dp_peer(offset), device_id_type=MESH)
+    pl.semaphore_wait(barrier, sections + dp_count - 2)
+
+    for offset in range(1, sections):
+        target = section_peer(offset)
+        remote(
+            piece_ref.at[target[0]],
+            weights.at[me_s, plane, core],
+            piece_send.at[offset - 1],
+            piece_recv.at[me_s],
+            target,
+        )
+    pltpu.make_async_copy(
+        piece_ref.at[me_s], weights.at[me_s, plane, core], piece_recv.at[me_s]
+    ).start()
+    for k in range(sections):
+        landed(weights.at[k, plane, core], piece_recv.at[k])
+        piece = weights.at[k, plane, core]
+        for offset in range(1, planes):
+            remote(
+                piece,
+                piece,
+                rail_send.at[k, offset - 1],
+                weight_recv.at[k, plane, core],
+                plane_peer(offset),
+            )
+        remote(piece, piece, core_send.at[k, 0], weight_recv.at[k, plane, core], partner)
+
+    def pass_on(k):
+        for offset in range(1, planes):
+            source = lax.rem(plane + offset, planes)
+            piece = weights.at[k, source, core]
+            landed(piece, weight_recv.at[k, source, core])
+            remote(
+                piece, piece, core_send.at[k, offset], weight_recv.at[k, source, core], partner
+            )
+
+    def arrive(k):
+        for source in range(planes):
+            landed(weights.at[k, source, other], weight_recv.at[k, source, other])
+
+    def weight_in(k):
+        return weights[k, :, :, :in_rows, :].reshape(width, rank)
+
+    def weight_out(k):
+        columns = [
+            weights[k, :, :, in_rows + out_rows * t : in_rows + out_rows * (t + 1), :].reshape(
+                rank, 128
+            )
+            for t in range(tiles)
+        ]
+        return jnp.concatenate(columns, axis=1)
+
+    def swap(slot, rows):
+        return [
+            remote(
+                sent.at[slot, pl.ds(0, rows)],
+                received.at[slot, offset - 1, pl.ds(0, rows)],
+                swap_send.at[slot, offset - 1],
+                swap_recv.at[slot, offset - 1],
+                section_peer(offset),
+            )
+            for offset in range(1, sections)
+        ]
+
+    def spread(column):
+        return jnp.transpose(jnp.broadcast_to(column, (tokens, tokens)))[:8]
+
+    streams[0] = stream_ref[...]
+    pass_on(0)
+    grad_partial = None
+    for k in range(sections):
+        last = k == sections - 1
+        arrive(k)
+        values = streams[k]
+        wide = values.astype(jnp.float32)
+        partial = dot(values, weight_in(k), 1, 0)
+        square = spread(jnp.sum(wide * wide, axis=1, keepdims=True))
+        square_hi = square.astype(jnp.bfloat16).astype(jnp.float32)
+        sent[k, :tokens] = partial.astype(jnp.bfloat16)
+        sent[k, tokens : tokens + 16] = jnp.concatenate(
+            [square_hi, square - square_hi], axis=0
+        ).astype(jnp.bfloat16)
+        rows = tokens + 16
+        if last:
+            grad_partial = dot(cotangent_ref[...], weight_out(k), 1, 1)
+            sent[k, rows : rows + tokens] = grad_partial.astype(jnp.bfloat16)
+            rows = rows + tokens
+        copies = swap(k, rows)
+        if not last:
+            pass_on(k + 1)
+        for offset, copy in enumerate(copies):
+            copy.wait_recv()
+            arrived = received[k, offset, : tokens + 16].astype(jnp.float32)
+            partial = partial + arrived[:tokens]
+            square = square + arrived[tokens : tokens + 8] + arrived[tokens + 8 : tokens + 16]
+            if last:
+                grad_partial = grad_partial + received[
+                    k, offset, tokens + 16 : rows
+                ].astype(jnp.float32)
+        mean = jnp.transpose(jnp.broadcast_to(square[:1], (tokens, tokens))) / channels
+        root = lax.rsqrt(mean + NORM_EPS)
+        pre_act = partial * root[:, :rank]
+        hidden = (pre_act * jax.nn.sigmoid(pre_act)).astype(jnp.bfloat16)
+        pre_acts[k] = pre_act
+        roots[k] = root
+        hiddens[k] = hidden
+        if not last:
+            streams[k + 1] = (wide + dot(hidden, weight_out(k), 1, 0)).astype(jnp.bfloat16)
+
+    def send_chip_sums(k):
+        landed(from_core.at[k], part_recv.at[k])
+        chip_sums[k] = (
+            parts[k, :, core].astype(jnp.float32) + from_core[k].astype(jnp.float32)
+        ).astype(jnp.bfloat16)
+        for offset in range(1, planes):
+            target = plane_peer(offset)
+            remote(
+                chip_sums.at[k, lax.rem(plane + offset, planes)],
+                from_planes.at[k, offset - 1],
+                sum_send.at[k, offset - 1],
+                sum_recv.at[k, offset - 1],
+                target,
+            )
+
+    grad = cotangent_ref[...].astype(jnp.float32)
+    for k in reversed(range(sections)):
+        slot = 2 * sections - 2 - k
+        pre_act = pre_acts[k]
+        root = roots[k]
+        squash = jax.nn.sigmoid(pre_act)
+        grad_act = grad_partial * squash * (1.0 + pre_act * (1.0 - squash))
+        act = grad_act.astype(jnp.bfloat16)
+        grad_rounded = grad.astype(jnp.bfloat16)
+        copies = []
+        if k > 0:
+            column = root[:, :1]
+            inner_mean = jnp.sum(grad_act * pre_act, axis=1, keepdims=True) / channels
+            grad_normed = dot(act, weight_in(k), 1, 1)
+            grad = grad + column * (
+                grad_normed - streams[k].astype(jnp.float32) * (column * inner_mean)
+            )
+            grad_partial = dot(grad.astype(jnp.bfloat16), weight_out(k - 1), 1, 1)
+            sent[slot + 1, :tokens] = grad_partial.astype(jnp.bfloat16)
+            copies = swap(slot + 1, tokens)
+        scaled = (grad_act * root[:, :rank]).astype(jnp.bfloat16)
+        part_in = dot(streams[k], scaled, 0, 0).astype(jnp.bfloat16)
+        parts[k, :, :, :in_rows, :] = part_in.reshape(planes, CORES, in_rows, rank)
+        part_out = dot(hiddens[k], grad_rounded, 0, 0).astype(jnp.bfloat16)
+        for t in range(tiles):
+            parts[k, :, :, in_rows + out_rows * t : in_rows + out_rows * (t + 1), :] = part_out[
+                :, 128 * t : 128 * (t + 1)
+            ].reshape(planes, CORES, out_rows, 128)
+        remote(parts.at[k, :, other], from_core.at[k], part_send.at[k], part_recv.at[k], partner)
+        if k < sections - 1:
+            send_chip_sums(k + 1)
+        for offset, copy in enumerate(copies):
+            copy.wait_recv()
+            grad_partial = grad_partial + received[slot + 1, offset, :tokens].astype(jnp.float32)
+    send_chip_sums(0)
+
+    for k in reversed(range(sections)):
+        total = chip_sums[k, plane].astype(jnp.float32)
+        for offset in range(1, planes):
+            landed(from_planes.at[k, offset - 1], sum_recv.at[k, offset - 1])
+            total = total + from_planes[k, offset - 1].astype(jnp.float32)
+        totals[k] = total.astype(jnp.bfloat16)
+
+        @pl.when(me_s != k)
+        def _():
+            pltpu.make_async_remote_copy(
+                src_ref=totals.at[k],
+                dst_ref=owned.at[me_s],
+                send_sem=total_send.at[k],
+                recv_sem=total_recv.at[me_s],
+                device_id=(k, me_d),
+                device_id_type=MESH,
+            ).start()
+
+        @pl.when(me_s == k)
+        def _():
+            pltpu.make_async_copy(totals.at[k], owned.at[me_s], total_recv.at[me_s]).start()
+
+    square = jnp.zeros((8, 128), jnp.float32)
+    for s in range(sections):
+        landed(owned.at[s], total_recv.at[s])
+        piece = owned[s].astype(jnp.float32)
+        in_part = piece[:in_rows] * gain_ref[s]
+        out_part = piece[in_rows:]
+        grad_ref[s, :in_rows] = in_part
+        grad_ref[s, in_rows:] = out_part
+        square = square + jnp.sum((in_part * in_part).reshape(-1, 8, 128), axis=0)
+        square = square + jnp.sum((out_part * out_part).reshape(-1, 8, 128), axis=0)
+    squares[0] = square
+    copies = [
+        remote(
+            squares.at[0],
+            squares_dp.at[offset - 1],
+            dp_send.at[offset - 1],
+            dp_recv.at[offset - 1],
+            dp_peer(offset),
+        )
+        for offset in range(1, dp_count)
+    ]
+    for offset, copy in enumerate(copies):
+        copy.wait_recv()
+        square = square + squares_dp[offset]
+    squares[1] = square
+    copies = [
+        remote(
+            squares.at[1],
+            squares_section.at[offset - 1],
+            section_send.at[offset - 1],
+            section_recv.at[offset - 1],
+            section_peer(offset),
+        )
+        for offset in range(1, sections)
+    ]
+    for offset, copy in enumerate(copies):
+        copy.wait_recv()
+        square = square + squares_section[offset]
+    count_all = 2.0 * channels * rank * sections
+    norm_total = jnp.sum(square, keepdims=True)
+    factor = jnp.minimum(1.0, lax.rsqrt(norm_total / count_all + CLIP_EPS))
+    factor_ref[...] = jnp.broadcast_to(factor, factor_ref.shape)
+
+    for copy in started:
+        copy.wait_send()
+    for k in range(sections):
+
+        @pl.when(me_s != k)
+        def _():
+            pltpu.make_async_copy(totals.at[k], totals.at[k], total_send.at[k]).wait()
+
+
+def fast_shards(
+    stream_in,
+    cotangent,
+    norm_gain,
+    weight_in,
+    weight_out,
+    moment_in,
+    variance_in,
+    moment_out,
+    variance_out,
+):
+    sections = lax.axis_size("section")
+    dp_count = lax.axis_size("dp")
+    planes = dp_count // CORES
+    place = lax.axis_index("section")
+    row = lax.axis_index("dp")
+    channels = stream_in.shape[-1]
+    tokens = stream_in.shape[0] * stream_in.shape[1]
+    shard_rows, rank = weight_in.shape[1:]
+    if tokens != rank:
+        return shards(
+            stream_in,
+            cotangent,
+            norm_gain,
+            weight_in,
+            weight_out,
+            moment_in,
+            variance_in,
+            moment_out,
+            variance_out,
+        )
+    out_rows = weight_out.shape[1]
+    in_rows = shard_rows // sections
+    width = channels // sections
+    tiles = width // 128
+    piece_rows = in_rows + out_rows * tiles
+
+    def own_channels(rows):
+        rows = rows.reshape(tokens, dp_count, sections, in_rows)
+        return lax.dynamic_index_in_dim(rows, place, 2, False).reshape(tokens, width)
+
+    gain = lax.dynamic_slice_in_dim(norm_gain[0], row * shard_rows, shard_rows).astype(jnp.float32)
+    gained = (weight_in[0].astype(jnp.float32) * gain[:, None]).astype(jnp.bfloat16)
+    out_cut = weight_out[0].reshape(out_rows, dp_count, sections, in_rows)
+    out_cut = out_cut.transpose(2, 0, 1, 3).reshape(sections, out_rows, tiles, 128)
+    out_cut = out_cut.transpose(0, 2, 1, 3).reshape(sections, tiles * out_rows, 128)
+    pieces = jnp.concatenate([gained.reshape(sections, in_rows, rank), out_cut], axis=1)
+
+    narrow, full = jnp.bfloat16, jnp.float32
+    slots = 2 * sections - 1
+    dma = pltpu.SemaphoreType.DMA
+    vmem = pl.BlockSpec(memory_space=pltpu.VMEM)
+    grads, factor = pl.pallas_call(
+        functools.partial(step_kernel, sections, planes),
+        out_shape=(
+            jax.ShapeDtypeStruct((sections, piece_rows, 128), full),
+            jax.ShapeDtypeStruct((8, 128), full),
+        ),
+        in_specs=[vmem] * 4,
+        out_specs=(vmem, vmem),
+        scratch_shapes=[
+            pltpu.VMEM((sections, planes, CORES, piece_rows, 128), narrow),
+            pltpu.VMEM((sections, planes, CORES, piece_rows, 128), narrow),
+            pltpu.VMEM((sections, planes, piece_rows, 128), narrow),
+            pltpu.VMEM((sections, planes, piece_rows, 128), narrow),
+            pltpu.VMEM((sections, planes - 1, piece_rows, 128), narrow),
+            pltpu.VMEM((sections, piece_rows, 128), narrow),
+            pltpu.VMEM((sections, piece_rows, 128), narrow),
+            pltpu.VMEM((sections, tokens, width), narrow),
+            pltpu.VMEM((sections, tokens, rank), full),
+            pltpu.VMEM((sections, tokens, tokens), full),
+            pltpu.VMEM((sections, tokens, rank), narrow),
+            pltpu.VMEM((slots, 2 * tokens + 16, rank), narrow),
+            pltpu.VMEM((slots, sections - 1, 2 * tokens + 16, rank), narrow),
+            pltpu.VMEM((2, 8, 128), full),
+            pltpu.VMEM((dp_count - 1, 8, 128), full),
+            pltpu.VMEM((sections - 1, 8, 128), full),
+            dma((sections - 1,)),
+            dma((sections,)),
+            dma((sections, planes - 1)),
+            dma((sections, planes)),
+            dma((sections, planes, CORES)),
+            dma((slots, sections - 1)),
+            dma((slots, sections - 1)),
+            dma((sections,)),
+            dma((sections,)),
+            dma((sections, planes - 1)),
+            dma((sections, planes - 1)),
+            dma((sections,)),
+            dma((sections,)),
+            dma((dp_count - 1,)),
+            dma((dp_count - 1,)),
+            dma((sections - 1,)),
+            dma((sections - 1,)),
+        ],
+        compiler_params=pltpu.CompilerParams(
+            collective_id=0, has_side_effects=True, vmem_limit_bytes=48 * 1024 * 1024
+        ),
+    )(
+        own_channels(stream_in),
+        own_channels(cotangent),
+        pieces,
+        gain.reshape(sections, in_rows, 1),
+    )
+    factor = factor[0, 0]
+    grad_w_in = grads[:, :in_rows].reshape(shard_rows, rank)
+    grad_w_out = grads[:, in_rows:].reshape(sections, tiles, out_rows, 128).transpose(0, 2, 1, 3)
+    grad_w_out = grad_w_out.reshape(sections, out_rows, dp_count, in_rows).transpose(1, 2, 0, 3)
+    grad_w_out = grad_w_out.reshape(out_rows, channels)
+    new_in, new_moment_in, new_variance_in = update(
+        weight_in[0], grad_w_in, moment_in[0], variance_in[0], factor
+    )
+    new_out, new_moment_out, new_variance_out = update(
+        weight_out[0], grad_w_out, moment_out[0], variance_out[0], factor
+    )
+    return (new_in, new_moment_in, new_variance_in, new_out, new_moment_out, new_variance_out)
+
+
+def aligned(sections, dp_count):
+    width, in_rows, out_rows = E // sections, E // (sections * dp_count), R // dp_count
+    return (
+        sections > 1
+        and dp_count % CORES == 0
+        and dp_count > CORES
+        and width % 128 == 0
+        and in_rows % 16 == 0
+        and out_rows % 16 == 0
+        and R == 128
+    )
+
+
 def solution(mesh):
+    fast = aligned(mesh.shape["section"], mesh.shape["dp"])
     return jax.shard_map(
-        shards,
+        fast_shards if fast else shards,
         mesh=mesh,
         in_specs=(
             P(None, "dp", None),

time: 358 us -> 92.8 us (0.26)
  waiting for transfers between devices: 183 us -> 0 us
  Pallas kernels: 0 us -> 75.5 us
  blocking collectives: 72.5 us -> 0 us
  starting transfers between devices: 29.6 us -> 0 us
  other arithmetic: 24.6 us -> 4.07 us
  between operations: 16.1 us -> 0.83 us
  local copies, waits for them, and re-layouts: 23.3 us -> 12.1 us
  matrix products: 7.27 us -> 0 us
    ppermute x10 -> x0, waiting for transfers between devices: 117 us -> none  [from_behind(): return lax.ppermute(x, axis, pairs)]
    pallas_call x0 -> x1, Pallas kernels: none -> 75.5 us  [fast_shards(): pl.pallas_call(functools.partial(step_kernel, sections, planes), out_shap...]
    reduce_scatter x2 -> x0, waiting for transfers between devices: 65.5 us -> none  [the longest x1 34.2 us: shards(): lax.psum_scatter(stacked_out.astype(jnp.bfloat16), 'dp', scatter_dimensio...]
    psum x1 -> x0, blocking collectives: 37.8 us -> none  [shards(): norm_total = lax.psum(local_sum, ('section', 'dp'))]
    all_gather x2 -> x0, blocking collectives: 34.7 us -> none  [the longest x1 17.8 us: shards(): lax.all_gather(in_slice, 'dp', axis=0, tiled=True)]
    ppermute x10 -> x0, starting transfers between devices: 29.5 us -> none  [from_behind(): return lax.ppermute(x, axis, pairs)]
    convert_element_type x10 -> x2, other arithmetic: 11.2 us -> 1.54 us  [the longest x1 1.42 us: fast_shards(): lax.dynamic_slice_in_dim(norm_gain[0], row * shard_rows, shard_rows)]
    cond x16 -> x0, local copies, waits for them, and re-layouts: 8.85 us -> none
  transfers between devices with their start and end apart: 12 -> 0, of which waited for: 12 -> 0; matrix products, arithmetic and copies ran while one was open for 1% -> 0% of each run, Pallas kernels for 0% -> 0%
where the time goes in v1:
time: 92.8 us; the launch traced here: 92.6 us
  Pallas kernels  75.5 us (81%)
  local copies, waits for them, and re-layouts  12.1 us (13%)
  other arithmetic  4.07 us (4%)
    pallas_call x1, Pallas kernels, fast_shards(): pl.pallas_call(functools.partial(step_kernel, sections, planes), out_shap...  75.5 us
    reshape x2, local copies, waits for them, and re-layouts, own_channels(): rows = rows.reshape(tokens, dp_count, sections, in_rows)  5.56 us
    unnamed x14, local copies, waits for them, and re-layouts  1.95 us
    dynamic_slice x3, local copies, waits for them, and re-layouts, own_channels(): lax.dynamic_index_in_dim(rows, place, 2, False).reshape(tokens, width)  1.93 us

profile of v1, /device:TPU:0, one launch (start us, length us, event | category | flops | bytes accessed | tf_op | source)
XLA Modules:
  0.0 92.6 jit_solution(13720796153447469952)
XLA Ops:
  0.6 0.0 copy-start
  0.6 4.1 %reshape.122 = bf16[128,8,4,112]{3,2,1,0:T(4,128)(2,1)S(1)} reshape(bf16[2,64,3584]{2,1,0:T(8,128)(2,1)} %param.9) | data formatting | bytes 1835008 | tf_op jit(solution)/shard_map/reshape | solution.py:586
  4.7 0.0 copy-done
  4.7 1.5 %reshape.124 = bf16[128,8,4,112]{3,2,1,0:T(4,128)(2,1)S(1)} reshape(bf16[2,64,3584]{2,1,0:T(8,128)(2,1)S(1)} %copy-done) | data formatting | bytes 1835008 | tf_op jit(solution)/shard_map/reshape | solution.py:586
  6.2 1.1 %constant_dynamic-slice_fusion = (bf16[128,8,1,112]{3,2,1,0:T(2,128)(2,1)S(1)}, bf16[128,8,1,112]{3,2,1,0:T(2,128)(2,1)S(1)}) fusion(bf16[128,8,4,112]{3,2,1,0:T(4,128)(2,1)S(1)} %reshape.124, s32[]{:T(128)S(6)} %select_n.8, bf16[128,8,4,112]{3,2,1,0:T(4,128)(2,1)S(1)} %reshape.122), kind=kLoop, calls=%fused_computation.16 | loop fusion | bytes 917508 | tf_op jit(solution)/shard_map/jit(dynamic_index_in_dim)/dynamic_slice | solution.py:587
  7.3 0.4 copy.25
  7.8 0.2 copy.29.stream_ref
  7.9 0.4 copy.26
  8.4 0.0 copy-start.1
  8.4 0.2 copy.30.cotangent_ref
  8.5 0.5 broadcast.87
  9.1 1.4 %fusion.6 = (f32[448]{0:T(512)S(1)}, f32[1,448]{1,0:T(1,128)S(1)}) fusion(f32[]{:T(128)} %broadcast.87, bf16[1,3584]{1,0:T(2,128)(2,1)} %param.11, s32[]{:T(128)S(6)} %select_n.9), kind=kLoop, calls=%fused_computation.18 | loop fusion | flops 448 | bytes 4488 | tf_op jit(solution)/shard_map/convert_element_type | solution.py:589
  10.5 0.1 reshape.130
  10.6 0.0 copy-done.1
  10.6 0.0 copy-start.2
  10.6 0.1 multiply_convert_fusion
  10.7 0.8 copy-done.2
  11.5 0.2 reshape_squeeze.3
  11.7 0.2 reshape.126
  11.9 0.2 reshape.134.gain_ref
  12.1 75.5 %shard_map.136 = (f32[4,224,128]{2,1,0:T(8,128)S(1)}, f32[8,128]{1,0:T(8,128)S(1)}) custom-call(bf16[128,896]{1,0:T(8,128)(2,1)S(1)} %copy.29.stream_ref, bf16[128,896]{1,0:T(8,128)(2,1)S(1)} %copy.30.cotangent_ref, bf16[4,224,128]{2,1,0:T(8,128)(2,1)S(1)} %pad_maximum_fusion.piece_ref, f32[4,112,1]{2,1,0:T(8,128)S(1)} %reshape.134.gain_ref), custom_call_target="tpu_custom_call" | custom-call | tf_op jit(solution)/shard_map/pallas_call | solution.py:600
  87.7 0.5 slice.9
  88.2 0.7 slice_multiply_fusion
  88.9 0.1 copy.36
  89.0 0.2 mul.209
  89.1 0.2 copy.33
  89.3 0.0 copy-start.3
  89.3 0.0 copy-start.4
  89.3 0.3 mul.211
  89.6 0.7 copy-done.3
  90.3 0.1 copy-done.4
  90.4 0.0 copy-start.5
  90.4 0.0 copy-start.6
  90.4 0.9 divide_subtract_fusion
  91.3 0.1 copy-done.5
  91.4 0.2 copy-done.6
  91.7 0.9 divide_subtract_fusion.1
  (3 shorter events, 0.1 us)
Async XLA Ops:
  0.6 4.1 %copy-start = (bf16[2,64,3584]{2,1,0:T(8,128)(2,1)S(1)}, bf16[2,64,3584]{2,1,0:T(8,128)(2,1)}, u32[]{:S(2)}) copy-start(bf16[2,64,3584]{2,1,0:T(8,128)(2,1)} %param.10) | copy-start | bytes 2752516
  8.4 2.2 %copy-start.1 = (bf16[1,448,128]{2,1,0:T(8,128)(2,1)S(1)}, bf16[1,448,128]{2,1,0:T(8,128)(2,1)}, u32[]{:S(2)}) copy-start(bf16[1,448,128]{2,1,0:T(8,128)(2,1)} %param.12) | copy-start | bytes 344068
  10.6 0.9 copy-start.2
  89.3 0.9 %copy-start.3 = (f32[1,16,3584]{2,1,0:T(8,128)S(1)}, f32[1,16,3584]{2,1,0:T(8,128)}, u32[]{:S(2)}) copy-start(f32[1,16,3584]{2,1,0:T(8,128)} %param.16) | copy-start | bytes 688132
  89.3 1.0 %copy-start.4 = (f32[1,16,3584]{2,1,0:T(8,128)S(1)}, f32[1,16,3584]{2,1,0:T(8,128)}, u32[]{:S(2)}) copy-start(f32[1,16,3584]{2,1,0:T(8,128)} %param.17) | copy-start | bytes 688132
  90.4 1.1 %copy-start.5 = (f32[1,448,128]{2,1,0:T(8,128)S(1)}, f32[1,448,128]{2,1,0:T(8,128)}, u32[]{:S(2)}) copy-start(f32[1,448,128]{2,1,0:T(8,128)} %param.14) | copy-start | bytes 688132
  90.4 1.3 %copy-start.6 = (f32[1,448,128]{2,1,0:T(8,128)S(1)}, f32[1,448,128]{2,1,0:T(8,128)}, u32[]{:S(2)}) copy-start(f32[1,448,128]{2,1,0:T(8,128)} %param.15) | copy-start | bytes 688132

commit v2 on v1

--- a/solution.py
+++ b/solution.py
@@ -226,11 +226,17 @@
     sections,
     planes,
     stream_ref,
+    cotangent_any,
+    gain_ref,
+    weight_in_ref,
+    weight_out_ref,
+    grad_in_ref,
+    grad_out_ref,
+    factor_ref,
+    rows_ref,
     cotangent_ref,
     piece_ref,
-    gain_ref,
-    grad_ref,
-    factor_ref,
+    gain_rows,
     weights,
     parts,
     from_core,
@@ -247,6 +253,7 @@
     squares,
     squares_dp,
     squares_section,
+    row_sems,
     piece_send,
     piece_recv,
     rail_send,
@@ -271,12 +278,12 @@
     core = lax.rem(me_d, CORES)
     other = 1 - core
     dp_count = planes * CORES
-    tokens, width = stream_ref.shape
+    tokens, width = cotangent_ref.shape
     channels = width * sections
-    rank = piece_ref.shape[2]
+    shard_rows, rank = weight_in_ref.shape
     tiles = width // 128
-    in_rows = gain_ref.shape[1]
-    out_rows = rank // dp_count
+    in_rows = shard_rows // sections
+    out_rows = weight_out_ref.shape[0]
 
     def section_peer(offset):
         return (lax.rem(me_s + offset, sections), me_d)
@@ -306,11 +313,50 @@
         pltpu.make_async_copy(target, target, sem).wait()
 
     started = []
+    row_copies = [
+        pltpu.make_async_copy(source, rows_ref.at[i], row_sems.at[i])
+        for i, source in enumerate((stream_ref, cotangent_any))
+    ]
+    for copy in row_copies:
+        copy.start()
     barrier = pltpu.get_barrier_semaphore()
     for offset in range(1, sections):
         pl.semaphore_signal(barrier, inc=1, device_id=section_peer(offset), device_id_type=MESH)
     for offset in range(1, dp_count):
         pl.semaphore_signal(barrier, inc=1, device_id=dp_peer(offset), device_id_type=MESH)
+
+    gain_tiles = gain_ref.shape[0]
+    gains = jnp.concatenate(
+        [gain_ref[...].astype(jnp.float32), jnp.zeros((128 - gain_tiles, 128), jnp.float32)], axis=0
+    )
+    gains = jnp.transpose(gains)
+    lanes = lax.broadcasted_iota(jnp.int32, (128, 128), 1)
+    for b in range(shard_rows // 64):
+        half = me_d * (shard_rows // 64) + b
+        column = jnp.sum(jnp.where(lanes == half // 2, gains, 0.0), axis=1, keepdims=True)
+        odd = jnp.full((64, 1), lax.rem(half, 2), jnp.int32) == 1
+        gain_rows[64 * b : 64 * (b + 1)] = jnp.broadcast_to(
+            jnp.where(odd, column[64:], column[:64]), (64, 128)
+        )
+
+    def own_channels(rows, s):
+        cuts = [
+            rows[:, shard_rows * d + in_rows * s : shard_rows * d + in_rows * (s + 1)]
+            for d in range(dp_count)
+        ]
+        return jnp.concatenate(cuts, axis=1)
+
+    shard_out = weight_out_ref[...].astype(jnp.float32)
+    for s in range(sections):
+        own = slice(in_rows * s, in_rows * (s + 1))
+        piece_ref[s, :in_rows] = (
+            weight_in_ref[own].astype(jnp.float32) * gain_rows[own]
+        ).astype(jnp.bfloat16)
+        cut = own_channels(shard_out, s).astype(jnp.bfloat16)
+        for t in range(tiles):
+            piece_ref[s, in_rows + out_rows * t : in_rows + out_rows * (t + 1)] = cut[
+                :, 128 * t : 128 * (t + 1)
+            ]
     pl.semaphore_wait(barrier, sections + dp_count - 2)
 
     for offset in range(1, sections):
@@ -378,7 +424,17 @@
     def spread(column):
         return jnp.transpose(jnp.broadcast_to(column, (tokens, tokens)))[:8]
 
-    streams[0] = stream_ref[...]
+    for copy in row_copies:
+        copy.wait()
+    for s in range(sections):
+
+        @pl.when(me_s == s)
+        def _():
+            streams[0] = own_channels(rows_ref[0].astype(jnp.float32), s).astype(jnp.bfloat16)
+            cotangent_ref[...] = own_channels(rows_ref[1].astype(jnp.float32), s).astype(
+                jnp.bfloat16
+            )
+
     pass_on(0)
     grad_partial = None
     for k in range(sections):
@@ -494,13 +550,19 @@
             pltpu.make_async_copy(totals.at[k], owned.at[me_s], total_recv.at[me_s]).start()
 
     square = jnp.zeros((8, 128), jnp.float32)
+    out_parts = []
     for s in range(sections):
         landed(owned.at[s], total_recv.at[s])
         piece = owned[s].astype(jnp.float32)
-        in_part = piece[:in_rows] * gain_ref[s]
+        own = slice(in_rows * s, in_rows * (s + 1))
+        in_part = piece[:in_rows] * gain_rows[own]
         out_part = piece[in_rows:]
-        grad_ref[s, :in_rows] = in_part
-        grad_ref[s, in_rows:] = out_part
+        grad_in_ref[own] = in_part
+        out_parts.append(
+            jnp.concatenate(
+                [out_part[out_rows * t : out_rows * (t + 1)] for t in range(tiles)], axis=1
+            )
+        )
         square = square + jnp.sum((in_part * in_part).reshape(-1, 8, 128), axis=0)
         square = square + jnp.sum((out_part * out_part).reshape(-1, 8, 128), axis=0)
     squares[0] = square
@@ -514,6 +576,14 @@
         )
         for offset in range(1, dp_count)
     ]
+    grad_out_ref[...] = jnp.concatenate(
+        [
+            out_parts[s][:, in_rows * d : in_rows * (d + 1)]
+            for d in range(dp_count)
+            for s in range(sections)
+        ],
+        axis=1,
+    )
     for offset, copy in enumerate(copies):
         copy.wait_recv()
         square = square + squares_dp[offset]
@@ -543,6 +613,15 @@
         @pl.when(me_s != k)
         def _():
             pltpu.make_async_copy(totals.at[k], totals.at[k], total_send.at[k]).wait()
+
+
+def adam_kernel(factor_ref, *refs):
+    factor = factor_ref[:1, :1]
+    for place in (0, 1):
+        weight, grad, moment, variance = (ref for ref in refs[4 * place : 4 * place + 4])
+        results = update(weight[0], grad[...], moment[0], variance[0], factor)
+        for ref, result in zip(refs[8 + 3 * place : 11 + 3 * place], results):
+            ref[...] = result
 
 
 def fast_shards(
@@ -559,8 +638,6 @@
     sections = lax.axis_size("section")
     dp_count = lax.axis_size("dp")
     planes = dp_count // CORES
-    place = lax.axis_index("section")
-    row = lax.axis_index("dp")
     channels = stream_in.shape[-1]
     tokens = stream_in.shape[0] * stream_in.shape[1]
     shard_rows, rank = weight_in.shape[1:]
@@ -582,30 +659,24 @@
     tiles = width // 128
     piece_rows = in_rows + out_rows * tiles
 
-    def own_channels(rows):
-        rows = rows.reshape(tokens, dp_count, sections, in_rows)
-        return lax.dynamic_index_in_dim(rows, place, 2, False).reshape(tokens, width)
-
-    gain = lax.dynamic_slice_in_dim(norm_gain[0], row * shard_rows, shard_rows).astype(jnp.float32)
-    gained = (weight_in[0].astype(jnp.float32) * gain[:, None]).astype(jnp.bfloat16)
-    out_cut = weight_out[0].reshape(out_rows, dp_count, sections, in_rows)
-    out_cut = out_cut.transpose(2, 0, 1, 3).reshape(sections, out_rows, tiles, 128)
-    out_cut = out_cut.transpose(0, 2, 1, 3).reshape(sections, tiles * out_rows, 128)
-    pieces = jnp.concatenate([gained.reshape(sections, in_rows, rank), out_cut], axis=1)
-
     narrow, full = jnp.bfloat16, jnp.float32
     slots = 2 * sections - 1
     dma = pltpu.SemaphoreType.DMA
     vmem = pl.BlockSpec(memory_space=pltpu.VMEM)
-    grads, factor = pl.pallas_call(
+    grad_w_in, grad_w_out, factor = pl.pallas_call(
         functools.partial(step_kernel, sections, planes),
         out_shape=(
-            jax.ShapeDtypeStruct((sections, piece_rows, 128), full),
+            jax.ShapeDtypeStruct((shard_rows, rank), full),
+            jax.ShapeDtypeStruct((out_rows, channels), full),
             jax.ShapeDtypeStruct((8, 128), full),
         ),
-        in_specs=[vmem] * 4,
-        out_specs=(vmem, vmem),
+        in_specs=[pl.BlockSpec(memory_space=pl.ANY)] * 2 + [vmem] * 3,
+        out_specs=(vmem, vmem, vmem),
         scratch_shapes=[
+            pltpu.VMEM((2, tokens, channels), narrow),
+            pltpu.VMEM((tokens, width), narrow),
+            pltpu.VMEM((sections, piece_rows, 128), narrow),
+            pltpu.VMEM((shard_rows, 128), full),
             pltpu.VMEM((sections, planes, CORES, piece_rows, 128), narrow),
             pltpu.VMEM((sections, planes, CORES, piece_rows, 128), narrow),
             pltpu.VMEM((sections, planes, piece_rows, 128), narrow),
@@ -622,6 +693,7 @@
             pltpu.VMEM((2, 8, 128), full),
             pltpu.VMEM((dp_count - 1, 8, 128), full),
             pltpu.VMEM((sections - 1, 8, 128), full),
+            dma((2,)),
             dma((sections - 1,)),
             dma((sections,)),
             dma((sections, planes - 1)),
@@ -644,23 +716,31 @@
             collective_id=0, has_side_effects=True, vmem_limit_bytes=48 * 1024 * 1024
         ),
     )(
-        own_channels(stream_in),
-        own_channels(cotangent),
-        pieces,
-        gain.reshape(sections, in_rows, 1),
-    )
-    factor = factor[0, 0]
-    grad_w_in = grads[:, :in_rows].reshape(shard_rows, rank)
-    grad_w_out = grads[:, in_rows:].reshape(sections, tiles, out_rows, 128).transpose(0, 2, 1, 3)
-    grad_w_out = grad_w_out.reshape(sections, out_rows, dp_count, in_rows).transpose(1, 2, 0, 3)
-    grad_w_out = grad_w_out.reshape(out_rows, channels)
-    new_in, new_moment_in, new_variance_in = update(
-        weight_in[0], grad_w_in, moment_in[0], variance_in[0], factor
-    )
-    new_out, new_moment_out, new_variance_out = update(
-        weight_out[0], grad_w_out, moment_out[0], variance_out[0], factor
-    )
-    return (new_in, new_moment_in, new_variance_in, new_out, new_moment_out, new_variance_out)
+        stream_in.reshape(tokens, channels),
+        cotangent.reshape(tokens, channels),
+        norm_gain.reshape(channels // 128, 128),
+        weight_in[0],
+        weight_out[0],
+    )
+    in_shape = jax.ShapeDtypeStruct(moment_in.shape, full)
+    out_shape = jax.ShapeDtypeStruct(moment_out.shape, full)
+    return pl.pallas_call(
+        adam_kernel,
+        out_shape=(in_shape,) * 3 + (out_shape,) * 3,
+        in_specs=[vmem] * 9,
+        out_specs=(vmem,) * 6,
+        compiler_params=pltpu.CompilerParams(vmem_limit_bytes=16 * 1024 * 1024),
+    )(
+        factor,
+        weight_in,
+        grad_w_in,
+        moment_in,
+        variance_in,
+        weight_out,
+        grad_w_out,
+        moment_out,
+        variance_out,
+    )
 
 
 def aligned(sections, dp_count):
@@ -673,6 +753,8 @@
         and in_rows % 16 == 0
         and out_rows % 16 == 0
         and R == 128
+        and E <= 128 * 128
+        and E % (64 * dp_count) == 0
     )
 
 

time: 92.8 us -> 83.1 us (0.90)
  local copies, waits for them, and re-layouts: 12.1 us -> 4.16 us
  other arithmetic: 4.07 us -> 0.76 us
  Pallas kernels: 75.5 us -> 77.2 us
    reshape x5 -> x0, local copies, waits for them, and re-layouts: 6.05 us -> none  [the longest x2 5.56 us: own_channels(): rows = rows.reshape(tokens, dp_count, sections, in_rows)]
    unnamed x14 -> x16, local copies, waits for them, and re-layouts: 1.95 us -> 4.16 us
    dynamic_slice x3 -> x0, local copies, waits for them, and re-layouts: 1.93 us -> none  [own_channels(): lax.dynamic_index_in_dim(rows, place, 2, False).reshape(tokens, width)]
    sub x2 -> x0, other arithmetic: 1.83 us -> none  [update(): weight.astype(jnp.float32)]
    convert_element_type x2 -> x0, other arithmetic: 1.54 us -> none  [the longest x1 1.42 us: fast_shards(): lax.dynamic_slice_in_dim(norm_gain[0], row * shard_rows, shard_rows)]
    pallas_call x0 -> x1, Pallas kernels: none -> 1.26 us  [fast_shards(): pl.pallas_call(adam_kernel, out_shape=(in_shape,) * 3 + (out_shape,) * 3,...]
where the time goes in v2:
time: 83.1 us; the launch traced here: 82.8 us
  Pallas kernels  77.2 us (93%)
  local copies, waits for them, and re-layouts  4.16 us (5%)
    pallas_call x1, Pallas kernels, fast_shards(): pl.pallas_call(functools.partial(step_kernel, sections, planes), out_shap...  75.9 us
    unnamed x16, local copies, waits for them, and re-layouts  4.16 us

profile of v2, /device:TPU:0, one launch (start us, length us, event | category | flops | bytes accessed | tf_op | source)
XLA Modules:
  0.0 82.8 jit_solution(16327614505756698177)
XLA Ops:
  0.6 0.8 reduce
  1.4 0.0 copy-start
  1.4 1.2 %copy-done = bf16[2,64,3584]{2,1,0:T(8,128)(2,1)S(1)} copy-done((bf16[2,64,3584]{2,1,0:T(8,128)(2,1)S(1)}, bf16[2,64,3584]{2,1,0:T(8,128)(2,1)}, u32[]{:S(2)}) %copy-start) | copy-done | bytes 917528
  2.6 0.0 copy-start.1
  2.6 1.2 %copy-done.1 = bf16[2,64,3584]{2,1,0:T(8,128)(2,1)S(1)} copy-done((bf16[2,64,3584]{2,1,0:T(8,128)(2,1)S(1)}, bf16[2,64,3584]{2,1,0:T(8,128)(2,1)}, u32[]{:S(2)}) %copy-start.1) | copy-done | bytes 917528
  3.8 0.0 copy-start.2
  3.8 0.9 %copy-done.2 = bf16[1,448,128]{2,1,0:T(8,128)(2,1)S(1)} copy-done((bf16[1,448,128]{2,1,0:T(8,128)(2,1)S(1)}, bf16[1,448,128]{2,1,0:T(8,128)(2,1)}, u32[]{:S(2)}) %copy-start.2) | copy-done | bytes 114712
  4.7 0.0 copy-start.3
  4.7 0.9 %copy-done.3 = bf16[1,16,3584]{2,1,0:T(8,128)(2,1)S(1)} copy-done((bf16[1,16,3584]{2,1,0:T(8,128)(2,1)S(1)}, bf16[1,16,3584]{2,1,0:T(8,128)(2,1)}, u32[]{:S(2)}) %copy-start.3) | copy-done | bytes 114712
  5.6 0.0 copy-start.4
  5.6 0.0 copy-start.5
  5.6 0.0 copy-start.6
  5.6 0.0 copy-start.7
  5.6 75.9 %shard_map.136 = (f32[448,128]{1,0:T(8,128)S(1)}, f32[16,3584]{1,0:T(8,128)S(1)}, f32[8,128]{1,0:T(8,128)S(1)}) custom-call(bf16[128,3584]{1,0:T(8,128)(2,1)S(1)} %bitcast.5, bf16[128,3584]{1,0:T(8,128)(2,1)S(1)} %bitcast.6, bf16[28,128]{1,0:T(8,128)(2,1)S(1)} %bitcast.9, bf16[448,128]{1,0:T(8,128)(2,1)S(1)} %bitcast.7, bf16[16,3584]{1,0:T(8,128)(2,1)S(1)} %bitcast.8), custom_call_target="tpu_custom_call" | custom-call | tf_op jit(solution)/shard_map/pallas_call | solution.py:666
  81.5 0.0 copy-done.4
  81.5 0.0 copy-done.5
  81.5 0.0 copy-done.6
  81.5 0.0 copy-done.7
  81.5 1.3 %shard_map.137 = (f32[1,448,128]{2,1,0:T(8,128)}, f32[1,448,128]{2,1,0:T(8,128)}, f32[1,448,128]{2,1,0:T(8,128)}, f32[1,16,3584]{2,1,0:T(8,128)}, f32[1,16,3584]{2,1,0:T(8,128)}, /*index=5*/f32[1,16,3584]{2,1,0:T(8,128)}) custom-call(f32[8,128]{1,0:T(8,128)S(1)} %get-tuple-element.9.factor_ref, bf16[1,448,128]{2,1,0:T(8,128)(2,1)S(1)} %copy-done.2, ...), custom_call_target="tpu_custom_call" | custom-call | tf_op jit(solution)/shard_map/pallas_call | solution.py:727
Async XLA Ops:
  1.4 1.2 %copy-start = (bf16[2,64,3584]{2,1,0:T(8,128)(2,1)S(1)}, bf16[2,64,3584]{2,1,0:T(8,128)(2,1)}, u32[]{:S(2)}) copy-start(bf16[2,64,3584]{2,1,0:T(8,128)(2,1)} %param.9) | copy-start | bytes 2752516
  2.6 1.2 %copy-start.1 = (bf16[2,64,3584]{2,1,0:T(8,128)(2,1)S(1)}, bf16[2,64,3584]{2,1,0:T(8,128)(2,1)}, u32[]{:S(2)}) copy-start(bf16[2,64,3584]{2,1,0:T(8,128)(2,1)} %param.10) | copy-start | bytes 2752516
  3.8 0.9 %copy-start.2 = (bf16[1,448,128]{2,1,0:T(8,128)(2,1)S(1)}, bf16[1,448,128]{2,1,0:T(8,128)(2,1)}, u32[]{:S(2)}) copy-start(bf16[1,448,128]{2,1,0:T(8,128)(2,1)} %refs_0_.1) | copy-start | bytes 344068
  4.7 0.9 %copy-start.3 = (bf16[1,16,3584]{2,1,0:T(8,128)(2,1)S(1)}, bf16[1,16,3584]{2,1,0:T(8,128)(2,1)}, u32[]{:S(2)}) copy-start(bf16[1,16,3584]{2,1,0:T(8,128)(2,1)} %refs_4_.1) | copy-start | bytes 344068
  5.6 75.9 %copy-start.4 = (f32[1,448,128]{2,1,0:T(8,128)S(1)}, f32[1,448,128]{2,1,0:T(8,128)}, u32[]{:S(2)}) copy-start(f32[1,448,128]{2,1,0:T(8,128)} %refs_2_.1) | copy-start | bytes 688132
  5.6 75.9 %copy-start.5 = (f32[1,448,128]{2,1,0:T(8,128)S(1)}, f32[1,448,128]{2,1,0:T(8,128)}, u32[]{:S(2)}) copy-start(f32[1,448,128]{2,1,0:T(8,128)} %refs_3_.1) | copy-start | bytes 688132
  5.6 75.9 %copy-start.6 = (f32[1,16,3584]{2,1,0:T(8,128)S(1)}, f32[1,16,3584]{2,1,0:T(8,128)}, u32[]{:S(2)}) copy-start(f32[1,16,3584]{2,1,0:T(8,128)} %refs_6_.1) | copy-start | bytes 688132
  5.6 75.9 %copy-start.7 = (f32[1,16,3584]{2,1,0:T(8,128)S(1)}, f32[1,16,3584]{2,1,0:T(8,128)}, u32[]{:S(2)}) copy-start(f32[1,16,3584]{2,1,0:T(8,128)} %refs_7_.1) | copy-start | bytes 688132

commit v3 on v2

--- a/solution.py
+++ b/solution.py
@@ -225,15 +225,18 @@
 def step_kernel(
     sections,
     planes,
-    stream_ref,
+    stream_any,
     cotangent_any,
-    gain_ref,
-    weight_in_ref,
-    weight_out_ref,
+    gain_any,
+    weight_in_any,
+    weight_out_any,
     grad_in_ref,
     grad_out_ref,
     factor_ref,
     rows_ref,
+    gain_ref,
+    weight_in_ref,
+    weight_out_ref,
     cotangent_ref,
     piece_ref,
     gain_rows,
@@ -253,10 +256,11 @@
     squares,
     squares_dp,
     squares_section,
-    row_sems,
+    load_sems,
     piece_send,
     piece_recv,
     rail_send,
+    relay_send,
     core_send,
     weight_recv,
     swap_send,
@@ -296,7 +300,7 @@
 
     partner = (me_s, plane * CORES + other)
 
-    def remote(source, target, send_sem, recv_sem, device):
+    def send(source, target, send_sem, recv_sem, device):
         copy = pltpu.make_async_remote_copy(
             src_ref=source,
             dst_ref=target,
@@ -306,18 +310,29 @@
             device_id_type=MESH,
         )
         copy.start()
-        started.append(copy)
         return copy
+
+    def remote(*copy):
+        started.append(send(*copy))
+        return started[-1]
 
     def landed(target, sem):
         pltpu.make_async_copy(target, target, sem).wait()
 
     started = []
-    row_copies = [
-        pltpu.make_async_copy(source, rows_ref.at[i], row_sems.at[i])
-        for i, source in enumerate((stream_ref, cotangent_any))
+    loads = [
+        pltpu.make_async_copy(source, target, load_sems.at[i])
+        for i, (source, target) in enumerate(
+            (
+                (gain_any, gain_ref),
+                (weight_out_any, weight_out_ref),
+                (weight_in_any, weight_in_ref),
+                (stream_any, rows_ref.at[0]),
+                (cotangent_any, rows_ref.at[1]),
+            )
+        )
     ]
-    for copy in row_copies:
+    for copy in loads:
         copy.start()
     barrier = pltpu.get_barrier_semaphore()
     for offset in range(1, sections):
@@ -325,10 +340,11 @@
     for offset in range(1, dp_count):
         pl.semaphore_signal(barrier, inc=1, device_id=dp_peer(offset), device_id_type=MESH)
 
-    gain_tiles = gain_ref.shape[0]
-    gains = jnp.concatenate(
-        [gain_ref[...].astype(jnp.float32), jnp.zeros((128 - gain_tiles, 128), jnp.float32)], axis=0
-    )
+    loads[0].wait()
+    gain_row = gain_ref[...].astype(jnp.float32)
+    gain_tiles = channels // 128
+    gains = [gain_row[:, 128 * t : 128 * (t + 1)] for t in range(gain_tiles)]
+    gains = jnp.concatenate(gains + [jnp.zeros((128 - gain_tiles, 128), jnp.float32)], axis=0)
     gains = jnp.transpose(gains)
     lanes = lax.broadcasted_iota(jnp.int32, (128, 128), 1)
     for b in range(shard_rows // 64):
@@ -346,6 +362,8 @@
         ]
         return jnp.concatenate(cuts, axis=1)
 
+    loads[1].wait()
+    loads[2].wait()
     shard_out = weight_out_ref[...].astype(jnp.float32)
     for s in range(sections):
         own = slice(in_rows * s, in_rows * (s + 1))
@@ -371,17 +389,24 @@
     pltpu.make_async_copy(
         piece_ref.at[me_s], weights.at[me_s, plane, core], piece_recv.at[me_s]
     ).start()
-    for k in range(sections):
+    far = planes - 1
+    for place in range(sections):
+        k = me_s if place == 0 else jnp.where(place - 1 < me_s, place - 1, place)
         landed(weights.at[k, plane, core], piece_recv.at[k])
         piece = weights.at[k, plane, core]
         for offset in range(1, planes):
-            remote(
-                piece,
-                piece,
-                rail_send.at[k, offset - 1],
-                weight_recv.at[k, plane, core],
-                plane_peer(offset),
-            )
+            target = lax.rem(plane + offset, planes)
+
+            @pl.when((target - plane != far) & (plane - target != far))
+            def _():
+                send(
+                    piece,
+                    piece,
+                    rail_send.at[k, offset - 1],
+                    weight_recv.at[k, plane, core],
+                    (me_s, target * CORES + core),
+                )
+
         remote(piece, piece, core_send.at[k, 0], weight_recv.at[k, plane, core], partner)
 
     def pass_on(k):
@@ -389,6 +414,23 @@
             source = lax.rem(plane + offset, planes)
             piece = weights.at[k, source, core]
             landed(piece, weight_recv.at[k, source, core])
+
+            @pl.when((source == 0) & (plane == far - 1))
+            def _():
+                send(
+                    piece,
+                    piece,
+                    relay_send.at[k, 0],
+                    weight_recv.at[k, source, core],
+                    (me_s, far * CORES + core),
+                )
+
+            @pl.when((source == far) & (plane == 1))
+            def _():
+                send(
+                    piece, piece, relay_send.at[k, 1], weight_recv.at[k, source, core], (me_s, core)
+                )
+
             remote(
                 piece, piece, core_send.at[k, offset], weight_recv.at[k, source, core], partner
             )
@@ -424,8 +466,8 @@
     def spread(column):
         return jnp.transpose(jnp.broadcast_to(column, (tokens, tokens)))[:8]
 
-    for copy in row_copies:
-        copy.wait()
+    loads[3].wait()
+    loads[4].wait()
     for s in range(sections):
 
         @pl.when(me_s == s)
@@ -476,30 +518,74 @@
         if not last:
             streams[k + 1] = (wide + dot(hidden, weight_out(k), 1, 0)).astype(jnp.bfloat16)
 
-    def send_chip_sums(k):
-        landed(from_core.at[k], part_recv.at[k])
-        chip_sums[k] = (
-            parts[k, :, core].astype(jnp.float32) + from_core[k].astype(jnp.float32)
+    def swap_part(unit):
+        remote(
+            parts.at[unit, :, other],
+            from_core.at[unit],
+            part_send.at[unit],
+            part_recv.at[unit],
+            partner,
+        )
+
+    def make_in_part(k, grad_act):
+        scaled = (grad_act * roots[k][:, :rank]).astype(jnp.bfloat16)
+        part = dot(streams[k], scaled, 0, 0).astype(jnp.bfloat16)
+        parts[2 * k] = part.reshape(planes, CORES, in_rows, rank)
+        swap_part(2 * k)
+
+    def make_out_part(k, grad_rounded):
+        part = dot(hiddens[k], grad_rounded, 0, 0).astype(jnp.bfloat16)
+        for t in range(tiles):
+            parts[2 * k + 1, :, :, out_rows * t : out_rows * (t + 1), :] = part[
+                :, 128 * t : 128 * (t + 1)
+            ].reshape(planes, CORES, out_rows, 128)
+        swap_part(2 * k + 1)
+
+    def send_chip_sums(unit):
+        landed(from_core.at[unit], part_recv.at[unit])
+        chip_sums[unit] = (
+            parts[unit, :, core].astype(jnp.float32) + from_core[unit].astype(jnp.float32)
         ).astype(jnp.bfloat16)
         for offset in range(1, planes):
-            target = plane_peer(offset)
             remote(
-                chip_sums.at[k, lax.rem(plane + offset, planes)],
-                from_planes.at[k, offset - 1],
-                sum_send.at[k, offset - 1],
-                sum_recv.at[k, offset - 1],
-                target,
+                chip_sums.at[unit, lax.rem(plane + offset, planes)],
+                from_planes.at[unit, offset - 1],
+                sum_send.at[unit, offset - 1],
+                sum_recv.at[unit, offset - 1],
+                plane_peer(offset),
             )
+
+    def send_total(unit):
+        k, kind = unit // 2, unit % 2
+        total = chip_sums[unit, plane].astype(jnp.float32)
+        for offset in range(1, planes):
+            landed(from_planes.at[unit, offset - 1], sum_recv.at[unit, offset - 1])
+            total = total + from_planes[unit, offset - 1].astype(jnp.float32)
+        totals[unit] = total.astype(jnp.bfloat16)
+        own = owned.at[kind, me_s]
+
+        @pl.when(me_s != k)
+        def _():
+            send(
+                totals.at[unit], own, total_send.at[unit], total_recv.at[kind, me_s], (k, me_d)
+            )
+
+        @pl.when(me_s == k)
+        def _():
+            pltpu.make_async_copy(totals.at[unit], own, total_recv.at[kind, me_s]).start()
+
+    def units_of(k):
+        units = [2 * k] + ([2 * k - 1] if k > 0 else [])
+        return [2 * k + 1] + units if k == sections - 1 else units
 
     grad = cotangent_ref[...].astype(jnp.float32)
     for k in reversed(range(sections)):
-        slot = 2 * sections - 2 - k
+        slot = 2 * sections - 1 - k
         pre_act = pre_acts[k]
         root = roots[k]
         squash = jax.nn.sigmoid(pre_act)
         grad_act = grad_partial * squash * (1.0 + pre_act * (1.0 - squash))
         act = grad_act.astype(jnp.bfloat16)
-        grad_rounded = grad.astype(jnp.bfloat16)
         copies = []
         if k > 0:
             column = root[:, :1]
@@ -508,55 +594,38 @@
             grad = grad + column * (
                 grad_normed - streams[k].astype(jnp.float32) * (column * inner_mean)
             )
-            grad_partial = dot(grad.astype(jnp.bfloat16), weight_out(k - 1), 1, 1)
-            sent[slot + 1, :tokens] = grad_partial.astype(jnp.bfloat16)
-            copies = swap(slot + 1, tokens)
-        scaled = (grad_act * root[:, :rank]).astype(jnp.bfloat16)
-        part_in = dot(streams[k], scaled, 0, 0).astype(jnp.bfloat16)
-        parts[k, :, :, :in_rows, :] = part_in.reshape(planes, CORES, in_rows, rank)
-        part_out = dot(hiddens[k], grad_rounded, 0, 0).astype(jnp.bfloat16)
-        for t in range(tiles):
-            parts[k, :, :, in_rows + out_rows * t : in_rows + out_rows * (t + 1), :] = part_out[
-                :, 128 * t : 128 * (t + 1)
-            ].reshape(planes, CORES, out_rows, 128)
-        remote(parts.at[k, :, other], from_core.at[k], part_send.at[k], part_recv.at[k], partner)
-        if k < sections - 1:
-            send_chip_sums(k + 1)
+            grad_rounded = grad.astype(jnp.bfloat16)
+            grad_partial = dot(grad_rounded, weight_out(k - 1), 1, 1)
+            sent[slot, :tokens] = grad_partial.astype(jnp.bfloat16)
+            copies = swap(slot, tokens)
+        if k == sections - 1:
+            make_out_part(k, cotangent_ref[...])
+        make_in_part(k, grad_act)
+        if k > 0:
+            make_out_part(k - 1, grad_rounded)
+        if k == 0 and sections > 2:
+            for unit in units_of(k + 2):
+                send_total(unit)
+        for unit in units_of(k):
+            send_chip_sums(unit)
+        if 0 < k < sections - 2:
+            for unit in units_of(k + 2):
+                send_total(unit)
         for offset, copy in enumerate(copies):
             copy.wait_recv()
-            grad_partial = grad_partial + received[slot + 1, offset, :tokens].astype(jnp.float32)
-    send_chip_sums(0)
-
-    for k in reversed(range(sections)):
-        total = chip_sums[k, plane].astype(jnp.float32)
-        for offset in range(1, planes):
-            landed(from_planes.at[k, offset - 1], sum_recv.at[k, offset - 1])
-            total = total + from_planes[k, offset - 1].astype(jnp.float32)
-        totals[k] = total.astype(jnp.bfloat16)
-
-        @pl.when(me_s != k)
-        def _():
-            pltpu.make_async_remote_copy(
-                src_ref=totals.at[k],
-                dst_ref=owned.at[me_s],
-                send_sem=total_send.at[k],
-                recv_sem=total_recv.at[me_s],
-                device_id=(k, me_d),
-                device_id_type=MESH,
-            ).start()
-
-        @pl.when(me_s == k)
-        def _():
-            pltpu.make_async_copy(totals.at[k], owned.at[me_s], total_recv.at[me_s]).start()
+            grad_partial = grad_partial + received[slot, offset, :tokens].astype(jnp.float32)
+    for k in (1, 0):
+        for unit in units_of(k):
+            send_total(unit)
 
     square = jnp.zeros((8, 128), jnp.float32)
     out_parts = []
     for s in range(sections):
-        landed(owned.at[s], total_recv.at[s])
-        piece = owned[s].astype(jnp.float32)
+        landed(owned.at[1, s], total_recv.at[1, s])
+        landed(owned.at[0, s], total_recv.at[0, s])
         own = slice(in_rows * s, in_rows * (s + 1))
-        in_part = piece[:in_rows] * gain_rows[own]
-        out_part = piece[in_rows:]
+        in_part = owned[0, s].astype(jnp.float32) * gain_rows[own]
+        out_part = owned[1, s].astype(jnp.float32)
         grad_in_ref[own] = in_part
         out_parts.append(
             jnp.concatenate(
@@ -609,18 +678,45 @@
     for copy in started:
         copy.wait_send()
     for k in range(sections):
+        for offset in range(1, planes):
+            target = lax.rem(plane + offset, planes)
+
+            @pl.when((target - plane != far) & (plane - target != far))
+            def _():
+                landed(weights.at[k, plane, core], rail_send.at[k, offset - 1])
+
+        @pl.when(plane == far - 1)
+        def _():
+            landed(weights.at[k, 0, core], relay_send.at[k, 0])
+
+        @pl.when(plane == 1)
+        def _():
+            landed(weights.at[k, far, core], relay_send.at[k, 1])
 
         @pl.when(me_s != k)
         def _():
-            pltpu.make_async_copy(totals.at[k], totals.at[k], total_send.at[k]).wait()
-
-
-def adam_kernel(factor_ref, *refs):
-    factor = factor_ref[:1, :1]
+            landed(totals.at[2 * k], total_send.at[2 * k])
+            landed(totals.at[2 * k + 1], total_send.at[2 * k + 1])
+
+
+def adam_kernel(factor_any, grad_in_any, grad_out_any, *refs):
+    inputs, outputs, loaded, sems = refs[:6], refs[6:12], refs[12:15], refs[15]
+    loads = [
+        pltpu.make_async_copy(source, target, sems.at[i])
+        for i, (source, target) in enumerate(
+            zip((factor_any, grad_in_any, grad_out_any), loaded)
+        )
+    ]
+    for copy in loads:
+        copy.start()
+    for copy in loads:
+        copy.wait()
+    factor = loaded[0][:1, :1]
     for place in (0, 1):
-        weight, grad, moment, variance = (ref for ref in refs[4 * place : 4 * place + 4])
-        results = update(weight[0], grad[...], moment[0], variance[0], factor)
-        for ref, result in zip(refs[8 + 3 * place : 11 + 3 * place], results):
+        weight, moment, variance = inputs[3 * place : 3 * place + 3]
+        grad = loaded[place + 1][...]
+        results = update(weight[0], grad, moment[0], variance[0], factor)
+        for ref, result in zip(outputs[3 * place : 3 * place + 3], results):
             ref[...] = result
 
 
@@ -661,6 +757,7 @@
 
     narrow, full = jnp.bfloat16, jnp.float32
     slots = 2 * sections - 1
+    units = 2 * sections
     dma = pltpu.SemaphoreType.DMA
     vmem = pl.BlockSpec(memory_space=pltpu.VMEM)
     grad_w_in, grad_w_out, factor = pl.pallas_call(
@@ -670,20 +767,23 @@
             jax.ShapeDtypeStruct((out_rows, channels), full),
             jax.ShapeDtypeStruct((8, 128), full),
         ),
-        in_specs=[pl.BlockSpec(memory_space=pl.ANY)] * 2 + [vmem] * 3,
+        in_specs=[pl.BlockSpec(memory_space=pl.ANY)] * 5,
         out_specs=(vmem, vmem, vmem),
         scratch_shapes=[
             pltpu.VMEM((2, tokens, channels), narrow),
+            pltpu.VMEM((1, channels), narrow),
+            pltpu.VMEM((shard_rows, rank), narrow),
+            pltpu.VMEM((out_rows, channels), narrow),
             pltpu.VMEM((tokens, width), narrow),
             pltpu.VMEM((sections, piece_rows, 128), narrow),
             pltpu.VMEM((shard_rows, 128), full),
             pltpu.VMEM((sections, planes, CORES, piece_rows, 128), narrow),
-            pltpu.VMEM((sections, planes, CORES, piece_rows, 128), narrow),
-            pltpu.VMEM((sections, planes, piece_rows, 128), narrow),
-            pltpu.VMEM((sections, planes, piece_rows, 128), narrow),
-            pltpu.VMEM((sections, planes - 1, piece_rows, 128), narrow),
-            pltpu.VMEM((sections, piece_rows, 128), narrow),
-            pltpu.VMEM((sections, piece_rows, 128), narrow),
+            pltpu.VMEM((units, planes, CORES, in_rows, 128), narrow),
+            pltpu.VMEM((units, planes, in_rows, 128), narrow),
+            pltpu.VMEM((units, planes, in_rows, 128), narrow),
+            pltpu.VMEM((units, planes - 1, in_rows, 128), narrow),
+            pltpu.VMEM((units, in_rows, 128), narrow),
+            pltpu.VMEM((2, sections, in_rows, 128), narrow),
             pltpu.VMEM((sections, tokens, width), narrow),
             pltpu.VMEM((sections, tokens, rank), full),
             pltpu.VMEM((sections, tokens, tokens), full),
@@ -693,32 +793,33 @@
             pltpu.VMEM((2, 8, 128), full),
             pltpu.VMEM((dp_count - 1, 8, 128), full),
             pltpu.VMEM((sections - 1, 8, 128), full),
-            dma((2,)),
+            dma((5,)),
             dma((sections - 1,)),
             dma((sections,)),
             dma((sections, planes - 1)),
+            dma((sections, 2)),
             dma((sections, planes)),
             dma((sections, planes, CORES)),
             dma((slots, sections - 1)),
             dma((slots, sections - 1)),
-            dma((sections,)),
-            dma((sections,)),
-            dma((sections, planes - 1)),
-            dma((sections, planes - 1)),
-            dma((sections,)),
-            dma((sections,)),
+            dma((units,)),
+            dma((units,)),
+            dma((units, planes - 1)),
+            dma((units, planes - 1)),
+            dma((units,)),
+            dma((2, sections)),
             dma((dp_count - 1,)),
             dma((dp_count - 1,)),
             dma((sections - 1,)),
             dma((sections - 1,)),
         ],
         compiler_params=pltpu.CompilerParams(
-            collective_id=0, has_side_effects=True, vmem_limit_bytes=48 * 1024 * 1024
+            collective_id=0, has_side_effects=True, vmem_limit_bytes=60 * 1024 * 1024
         ),
     )(
         stream_in.reshape(tokens, channels),
         cotangent.reshape(tokens, channels),
-        norm_gain.reshape(channels // 128, 128),
+        norm_gain,
         weight_in[0],
         weight_out[0],
     )
@@ -727,17 +828,23 @@
     return pl.pallas_call(
         adam_kernel,
         out_shape=(in_shape,) * 3 + (out_shape,) * 3,
-        in_specs=[vmem] * 9,
+        in_specs=[pl.BlockSpec(memory_space=pl.ANY)] * 3 + [vmem] * 6,
         out_specs=(vmem,) * 6,
+        scratch_shapes=[
+            pltpu.VMEM((8, 128), full),
+            pltpu.VMEM((shard_rows, rank), full),
+            pltpu.VMEM((out_rows, channels), full),
+            dma((3,)),
+        ],
         compiler_params=pltpu.CompilerParams(vmem_limit_bytes=16 * 1024 * 1024),
     )(
         factor,
+        grad_w_in,
+        grad_w_out,
         weight_in,
-        grad_w_in,
         moment_in,
         variance_in,
         weight_out,
-        grad_w_out,
         moment_out,
         variance_out,
     )
@@ -748,7 +855,7 @@
     return (
         sections > 1
         and dp_count % CORES == 0
-        and dp_count > CORES
+        and dp_count > 2 * CORES
         and width % 128 == 0
         and in_rows % 16 == 0
         and out_rows % 16 == 0

time: 83.1 us -> 75.5 us (0.909)
  Pallas kernels: 77.2 us -> 72.1 us
  local copies, waits for them, and re-layouts: 4.16 us -> 2.5 us
    pallas_call x1, Pallas kernels: 75.9 us -> 70.2 us  [fast_shards(): pl.pallas_call(functools.partial(step_kernel, sections, planes), out_shap...]
    unnamed x16 -> x18, local copies, waits for them, and re-layouts: 4.16 us -> 2.5 us
where the time goes in v3:
time: 75.5 us; the launch traced here: 75.3 us
  Pallas kernels  72.1 us (95%)
  local copies, waits for them, and re-layouts  2.5 us (3%)
    pallas_call x1, Pallas kernels, fast_shards(): pl.pallas_call(functools.partial(step_kernel, sections, planes), out_shap...  70.2 us
    unnamed x18, local copies, waits for them, and re-layouts  2.5 us
    pallas_call x1, Pallas kernels, fast_shards(): pl.pallas_call(adam_kernel, out_shape=(in_shape,) * 3 + (out_shape,) * 3,...  1.85 us

profile of v3, /device:TPU:0, one launch (start us, length us, event | category | flops | bytes accessed | tf_op | source)
XLA Modules:
  0.0 75.3 jit_solution(11483818322257634875)
XLA Ops:
  0.6 0.0 copy-start
  0.6 0.0 copy-start.1
  0.7 0.0 copy-start.2
  0.7 0.0 copy-start.3
  0.7 0.0 copy-start.4
  0.7 0.0 copy-start.5
  0.7 70.2 %shard_map.136 = (f32[448,128]{1,0:T(8,128)}, f32[16,3584]{1,0:T(8,128)}, f32[8,128]{1,0:T(8,128)}) custom-call(bf16[128,3584]{1,0:T(8,128)(2,1)} %bitcast.6, bf16[128,3584]{1,0:T(8,128)(2,1)} %bitcast.7, bf16[1,3584]{1,0:T(2,128)(2,1)} %gain_any.1, bf16[448,128]{1,0:T(8,128)(2,1)} %bitcast.4, bf16[16,3584]{1,0:T(8,128)(2,1)} %bitcast.5), custom_call_target="tpu_custom_call" | custom-call | tf_op jit(solution)/shard_map/pallas_call | solution.py:763
  70.9 0.0 copy-start.8
  70.9 0.0 copy-done
  70.9 0.0 copy-done.1
  70.9 0.0 copy-done.2
  71.0 0.0 copy-done.3
  71.0 0.0 copy-done.4
  71.0 0.0 copy-done.5
  71.0 0.6 copy-done.8
  71.6 0.0 copy-start.6
  71.6 0.9 %copy-done.6 = f32[448,128]{1,0:T(8,128)S(1)} copy-done((f32[448,128]{1,0:T(8,128)S(1)}, f32[448,128]{1,0:T(8,128)}, u32[]{:S(2)}) %copy-start.6) | copy-done | bytes 229400
  72.5 0.0 copy-start.7
  72.5 0.9 %copy-done.7 = f32[16,3584]{1,0:T(8,128)S(1)} copy-done((f32[16,3584]{1,0:T(8,128)S(1)}, f32[16,3584]{1,0:T(8,128)}, u32[]{:S(2)}) %copy-start.7) | copy-done | bytes 229400
  73.5 1.9 %shard_map.137 = (f32[1,448,128]{2,1,0:T(8,128)}, f32[1,448,128]{2,1,0:T(8,128)}, f32[1,448,128]{2,1,0:T(8,128)}, f32[1,16,3584]{2,1,0:T(8,128)}, f32[1,16,3584]{2,1,0:T(8,128)}, /*index=5*/f32[1,16,3584]{2,1,0:T(8,128)}) custom-call(f32[8,128]{1,0:T(8,128)S(1)} %copy-done.8, f32[448,128]{1,0:T(8,128)S(1)} %copy-done.6, f32[16,3584]{1,0:T(8,128)S(1)} %copy-done.7, ...), custom_call_target="tpu_custom_call" | custom-call | tf_op jit(solution)/shard_map/pallas_call | solution.py:828
Async XLA Ops:
  0.6 70.3 %copy-start = (bf16[1,448,128]{2,1,0:T(8,128)(2,1)S(1)}, bf16[1,448,128]{2,1,0:T(8,128)(2,1)}, u32[]{:S(2)}) copy-start(bf16[1,448,128]{2,1,0:T(8,128)(2,1)} %refs_0_.1) | copy-start | bytes 344068
  0.6 70.3 %copy-start.1 = (bf16[1,16,3584]{2,1,0:T(8,128)(2,1)S(1)}, bf16[1,16,3584]{2,1,0:T(8,128)(2,1)}, u32[]{:S(2)}) copy-start(bf16[1,16,3584]{2,1,0:T(8,128)(2,1)} %refs_3_.1) | copy-start | bytes 344068
  0.7 70.3 %copy-start.2 = (f32[1,448,128]{2,1,0:T(8,128)S(1)}, f32[1,448,128]{2,1,0:T(8,128)}, u32[]{:S(2)}) copy-start(f32[1,448,128]{2,1,0:T(8,128)} %refs_1_.1) | copy-start | bytes 688132
  0.7 70.3 %copy-start.3 = (f32[1,448,128]{2,1,0:T(8,128)S(1)}, f32[1,448,128]{2,1,0:T(8,128)}, u32[]{:S(2)}) copy-start(f32[1,448,128]{2,1,0:T(8,128)} %refs_2_.1) | copy-start | bytes 688132
  0.7 70.3 %copy-start.4 = (f32[1,16,3584]{2,1,0:T(8,128)S(1)}, f32[1,16,3584]{2,1,0:T(8,128)}, u32[]{:S(2)}) copy-start(f32[1,16,3584]{2,1,0:T(8,128)} %refs_4_.1) | copy-start | bytes 688132
  0.7 70.3 %copy-start.5 = (f32[1,16,3584]{2,1,0:T(8,128)S(1)}, f32[1,16,3584]{2,1,0:T(8,128)}, u32[]{:S(2)}) copy-start(f32[1,16,3584]{2,1,0:T(8,128)} %refs_5_.1) | copy-start | bytes 688132
  70.9 0.7 copy-start.8
  71.6 0.9 %copy-start.6 = (f32[448,128]{1,0:T(8,128)S(1)}, f32[448,128]{1,0:T(8,128)}, u32[]{:S(2)}) copy-start(f32[448,128]{1,0:T(8,128)} %get-tuple-element.10.grad_in_any) | copy-start | bytes 688132
  72.5 0.9 %copy-start.7 = (f32[16,3584]{1,0:T(8,128)S(1)}, f32[16,3584]{1,0:T(8,128)}, u32[]{:S(2)}) copy-start(f32[16,3584]{1,0:T(8,128)} %get-tuple-element.11.grad_out_any) | copy-start | bytes 688132

commit v4 on v3

--- a/solution.py
+++ b/solution.py
@@ -240,6 +240,8 @@
     cotangent_ref,
     piece_ref,
     gain_rows,
+    gain_sent,
+    gain_of,
     weights,
     parts,
     from_core,
@@ -257,6 +259,8 @@
     squares_dp,
     squares_section,
     load_sems,
+    gain_send,
+    gain_recv,
     piece_send,
     piece_recv,
     rail_send,
@@ -408,6 +412,19 @@
                 )
 
         remote(piece, piece, core_send.at[k, 0], weight_recv.at[k, plane, core], partner)
+
+    for s in range(sections):
+        gain_sent[s] = gain_rows[in_rows * s : in_rows * (s + 1)].astype(jnp.bfloat16)
+    for offset in range(1, sections):
+        target = section_peer(offset)
+        remote(
+            gain_sent.at[target[0]],
+            gain_of.at[me_s],
+            gain_send.at[offset - 1],
+            gain_recv.at[me_s],
+            target,
+        )
+    pltpu.make_async_copy(gain_sent.at[me_s], gain_of.at[me_s], gain_recv.at[me_s]).start()
 
     def pass_on(k):
         for offset in range(1, planes):
@@ -561,7 +578,8 @@
         for offset in range(1, planes):
             landed(from_planes.at[unit, offset - 1], sum_recv.at[unit, offset - 1])
             total = total + from_planes[unit, offset - 1].astype(jnp.float32)
-        totals[unit] = total.astype(jnp.bfloat16)
+        total = total.astype(jnp.bfloat16)
+        totals[unit] = total
         own = owned.at[kind, me_s]
 
         @pl.when(me_s != k)
@@ -574,10 +592,18 @@
         def _():
             pltpu.make_async_copy(totals.at[unit], own, total_recv.at[kind, me_s]).start()
 
+        grad_total = total.astype(jnp.float32)
+        if kind == 0:
+            grad_total = grad_total * gain_of[k].astype(jnp.float32)
+        return jnp.sum((grad_total * grad_total).reshape(-1, 8, 128), axis=0)
+
     def units_of(k):
         units = [2 * k] + ([2 * k - 1] if k > 0 else [])
         return [2 * k + 1] + units if k == sections - 1 else units
 
+    for k in range(sections):
+        landed(gain_of.at[k], gain_recv.at[k])
+    square = jnp.zeros((8, 128), jnp.float32)
     grad = cotangent_ref[...].astype(jnp.float32)
     for k in reversed(range(sections)):
         slot = 2 * sections - 1 - k
@@ -605,20 +631,30 @@
             make_out_part(k - 1, grad_rounded)
         if k == 0 and sections > 2:
             for unit in units_of(k + 2):
-                send_total(unit)
+                square = square + send_total(unit)
         for unit in units_of(k):
             send_chip_sums(unit)
         if 0 < k < sections - 2:
             for unit in units_of(k + 2):
-                send_total(unit)
+                square = square + send_total(unit)
         for offset, copy in enumerate(copies):
             copy.wait_recv()
             grad_partial = grad_partial + received[slot, offset, :tokens].astype(jnp.float32)
     for k in (1, 0):
         for unit in units_of(k):
-            send_total(unit)
-
-    square = jnp.zeros((8, 128), jnp.float32)
+            square = square + send_total(unit)
+
+    squares[0] = square
+    copies = [
+        remote(
+            squares.at[0],
+            squares_dp.at[offset - 1],
+            dp_send.at[offset - 1],
+            dp_recv.at[offset - 1],
+            dp_peer(offset),
+        )
+        for offset in range(1, dp_count)
+    ]
     out_parts = []
     for s in range(sections):
         landed(owned.at[1, s], total_recv.at[1, s])
@@ -632,19 +668,6 @@
                 [out_part[out_rows * t : out_rows * (t + 1)] for t in range(tiles)], axis=1
             )
         )
-        square = square + jnp.sum((in_part * in_part).reshape(-1, 8, 128), axis=0)
-        square = square + jnp.sum((out_part * out_part).reshape(-1, 8, 128), axis=0)
-    squares[0] = square
-    copies = [
-        remote(
-            squares.at[0],
-            squares_dp.at[offset - 1],
-            dp_send.at[offset - 1],
-            dp_recv.at[offset - 1],
-            dp_peer(offset),
-        )
-        for offset in range(1, dp_count)
-    ]
     grad_out_ref[...] = jnp.concatenate(
         [
             out_parts[s][:, in_rows * d : in_rows * (d + 1)]
@@ -699,25 +722,29 @@
             landed(totals.at[2 * k + 1], total_send.at[2 * k + 1])
 
 
-def adam_kernel(factor_any, grad_in_any, grad_out_any, *refs):
-    inputs, outputs, loaded, sems = refs[:6], refs[6:12], refs[12:15], refs[15]
+def adam_kernel(*refs):
+    inputs, outputs, loaded, results = refs[:9], refs[9:15], refs[15:24], refs[24:30]
+    load_sems, store_sems = refs[30:]
     loads = [
-        pltpu.make_async_copy(source, target, sems.at[i])
-        for i, (source, target) in enumerate(
-            zip((factor_any, grad_in_any, grad_out_any), loaded)
-        )
+        pltpu.make_async_copy(inputs[i], loaded[i], load_sems.at[i]) for i in range(len(inputs))
     ]
     for copy in loads:
         copy.start()
-    for copy in loads:
-        copy.wait()
+    stores = []
+    loads[0].wait()
     factor = loaded[0][:1, :1]
     for place in (0, 1):
-        weight, moment, variance = inputs[3 * place : 3 * place + 3]
-        grad = loaded[place + 1][...]
-        results = update(weight[0], grad, moment[0], variance[0], factor)
-        for ref, result in zip(outputs[3 * place : 3 * place + 3], results):
-            ref[...] = result
+        for copy in loads[4 * place + 1 : 4 * place + 5]:
+            copy.wait()
+        grad, weight, moment, variance = loaded[4 * place + 1 : 4 * place + 5]
+        updated = update(weight[0], grad[...], moment[0], variance[0], factor)
+        for i, result in enumerate(updated, start=3 * place):
+            results[i][...] = result
+            copy = pltpu.make_async_copy(results[i], outputs[i], store_sems.at[i])
+            copy.start()
+            stores.append(copy)
+    for copy in stores:
+        copy.wait()
 
 
 def fast_shards(
@@ -777,6 +804,8 @@
             pltpu.VMEM((tokens, width), narrow),
             pltpu.VMEM((sections, piece_rows, 128), narrow),
             pltpu.VMEM((shard_rows, 128), full),
+            pltpu.VMEM((sections, in_rows, 128), narrow),
+            pltpu.VMEM((sections, in_rows, 128), narrow),
             pltpu.VMEM((sections, planes, CORES, piece_rows, 128), narrow),
             pltpu.VMEM((units, planes, CORES, in_rows, 128), narrow),
             pltpu.VMEM((units, planes, in_rows, 128), narrow),
@@ -794,6 +823,8 @@
             pltpu.VMEM((dp_count - 1, 8, 128), full),
             pltpu.VMEM((sections - 1, 8, 128), full),
             dma((5,)),
+            dma((sections - 1,)),
+            dma((sections,)),
             dma((sections - 1,)),
             dma((sections,)),
             dma((sections, planes - 1)),
@@ -825,29 +856,31 @@
     )
     in_shape = jax.ShapeDtypeStruct(moment_in.shape, full)
     out_shape = jax.ShapeDtypeStruct(moment_out.shape, full)
+    arrays = (
+        factor,
+        grad_w_in,
+        weight_in,
+        moment_in,
+        variance_in,
+        grad_w_out,
+        weight_out,
+        moment_out,
+        variance_out,
+    )
+    anywhere = pl.BlockSpec(memory_space=pl.ANY)
     return pl.pallas_call(
         adam_kernel,
         out_shape=(in_shape,) * 3 + (out_shape,) * 3,
-        in_specs=[pl.BlockSpec(memory_space=pl.ANY)] * 3 + [vmem] * 6,
-        out_specs=(vmem,) * 6,
+        in_specs=[anywhere] * len(arrays),
+        out_specs=(anywhere,) * 6,
         scratch_shapes=[
-            pltpu.VMEM((8, 128), full),
-            pltpu.VMEM((shard_rows, rank), full),
-            pltpu.VMEM((out_rows, channels), full),
-            dma((3,)),
+            *(pltpu.VMEM(array.shape, array.dtype) for array in arrays),
+            *(pltpu.VMEM(shape.shape, full) for shape in (in_shape,) * 3 + (out_shape,) * 3),
+            dma((len(arrays),)),
+            dma((6,)),
         ],
-        compiler_params=pltpu.CompilerParams(vmem_limit_bytes=16 * 1024 * 1024),
-    )(
-        factor,
-        grad_w_in,
-        grad_w_out,
-        weight_in,
-        moment_in,
-        variance_in,
-        weight_out,
-        moment_out,
-        variance_out,
-    )
+        compiler_params=pltpu.CompilerParams(vmem_limit_bytes=60 * 1024 * 1024),
+    )(*arrays)
 
 
 def aligned(sections, dp_count):

time: 75.5 us -> 72.5 us (0.960)
  local copies, waits for them, and re-layouts: 2.5 us -> 0 us
    unnamed x18 -> x0, local copies, waits for them, and re-layouts: 2.5 us -> none
    pallas_call x1, Pallas kernels: 70.2 us -> 68.9 us  [fast_shards(): pl.pallas_call(functools.partial(step_kernel, sections, planes), out_shap...]
    pallas_call x1, Pallas kernels: 1.85 us -> 2.66 us  [fast_shards(): pl.pallas_call(adam_kernel, out_shape=(in_shape,) * 3 + (out_shape,) * 3,...]
where the time goes in v4:
time: 72.5 us; the launch traced here: 72.2 us
  Pallas kernels  71.6 us (99%)
    pallas_call x1, Pallas kernels, fast_shards(): pl.pallas_call(functools.partial(step_kernel, sections, planes), out_shap...  68.9 us
    pallas_call x1, Pallas kernels, fast_shards(): pl.pallas_call(adam_kernel, out_shape=(in_shape,) * 3 + (out_shape,) * 3,...  2.66 us

profile of v4, /device:TPU:0, one launch (start us, length us, event | category | flops | bytes accessed | tf_op | source)
XLA Modules:
  0.0 72.2 jit_solution(13996223174479185407)
XLA Ops:
  0.6 68.9 %shard_map.136 = (f32[448,128]{1,0:T(8,128)}, f32[16,3584]{1,0:T(8,128)}, f32[8,128]{1,0:T(8,128)}) custom-call(bf16[128,3584]{1,0:T(8,128)(2,1)} %bitcast.4, bf16[128,3584]{1,0:T(8,128)(2,1)} %bitcast.5, bf16[1,3584]{1,0:T(2,128)(2,1)} %gain_any.1, bf16[448,128]{1,0:T(8,128)(2,1)} %bitcast.6, bf16[16,3584]{1,0:T(8,128)(2,1)} %bitcast.7), custom_call_target="tpu_custom_call" | custom-call | tf_op jit(solution)/shard_map/pallas_call | solution.py:790
  69.6 2.7 %shard_map.137 = (f32[1,448,128]{2,1,0:T(8,128)}, f32[1,448,128]{2,1,0:T(8,128)}, f32[1,448,128]{2,1,0:T(8,128)}, f32[1,16,3584]{2,1,0:T(8,128)}, f32[1,16,3584]{2,1,0:T(8,128)}, /*index=5*/f32[1,16,3584]{2,1,0:T(8,128)}) custom-call(f32[8,128]{1,0:T(8,128)} %get-tuple-element.9.refs_0_, f32[448,128]{1,0:T(8,128)} %get-tuple-element.10.refs_1_, ...), custom_call_target="tpu_custom_call" | custom-call | tf_op jit(solution)/shard_map/pallas_call | solution.py:871

commit v5 on v4

--- a/solution.py
+++ b/solution.py
@@ -214,6 +214,7 @@
 
 MESH = pl.DeviceIdType.MESH
 CORES = 2
+HALVES = 2
 
 
 def dot(left, right, left_dim, right_dim):
@@ -255,6 +256,8 @@
     hiddens,
     sent,
     received,
+    sent_halves,
+    received_halves,
     squares,
     squares_dp,
     squares_section,
@@ -269,6 +272,8 @@
     weight_recv,
     swap_send,
     swap_recv,
+    half_send,
+    half_recv,
     part_send,
     part_recv,
     sum_send,
@@ -494,46 +499,76 @@
                 jnp.bfloat16
             )
 
-    pass_on(0)
-    grad_partial = None
-    for k in range(sections):
-        last = k == sections - 1
-        arrive(k)
-        values = streams[k]
+    half = tokens // HALVES
+
+    def forward_send(k, h):
+        rows = slice(half * h, half * (h + 1))
+        values = streams[k, rows]
         wide = values.astype(jnp.float32)
         partial = dot(values, weight_in(k), 1, 0)
-        square = spread(jnp.sum(wide * wide, axis=1, keepdims=True))
+        square = jnp.sum(wide * wide, axis=1, keepdims=True)
+        square = spread(jnp.concatenate([square, jnp.zeros((tokens - half, 1), jnp.float32)], axis=0))
         square_hi = square.astype(jnp.bfloat16).astype(jnp.float32)
-        sent[k, :tokens] = partial.astype(jnp.bfloat16)
-        sent[k, tokens : tokens + 16] = jnp.concatenate(
+        sent_half = sent_halves.at[HALVES * k + h]
+        sent_half[:half] = partial.astype(jnp.bfloat16)
+        sent_half[half : half + 16] = jnp.concatenate(
             [square_hi, square - square_hi], axis=0
         ).astype(jnp.bfloat16)
-        rows = tokens + 16
-        if last:
-            grad_partial = dot(cotangent_ref[...], weight_out(k), 1, 1)
-            sent[k, rows : rows + tokens] = grad_partial.astype(jnp.bfloat16)
-            rows = rows + tokens
-        copies = swap(k, rows)
-        if not last:
-            pass_on(k + 1)
+        count = half + 16
+        grad_part = None
+        if k == sections - 1:
+            grad_part = dot(cotangent_ref[rows], weight_out(k), 1, 1)
+            sent_half[count : count + half] = grad_part.astype(jnp.bfloat16)
+            count = count + half
+        copies = [
+            remote(
+                sent_half.at[pl.ds(0, count)],
+                received_halves.at[HALVES * k + h, offset - 1, pl.ds(0, count)],
+                half_send.at[HALVES * k + h, offset - 1],
+                half_recv.at[HALVES * k + h, offset - 1],
+                section_peer(offset),
+            )
+            for offset in range(1, sections)
+        ]
+        return copies, partial, square, grad_part
+
+    def forward_receive(k, h, state):
+        rows = slice(half * h, half * (h + 1))
+        copies, partial, square, grad_part = state
         for offset, copy in enumerate(copies):
             copy.wait_recv()
-            arrived = received[k, offset, : tokens + 16].astype(jnp.float32)
-            partial = partial + arrived[:tokens]
-            square = square + arrived[tokens : tokens + 8] + arrived[tokens + 8 : tokens + 16]
-            if last:
-                grad_partial = grad_partial + received[
-                    k, offset, tokens + 16 : rows
-                ].astype(jnp.float32)
-        mean = jnp.transpose(jnp.broadcast_to(square[:1], (tokens, tokens))) / channels
+            count = half + 16 + (0 if grad_part is None else half)
+            arrived = received_halves[HALVES * k + h, offset, :count].astype(jnp.float32)
+            partial = partial + arrived[:half]
+            square = square + arrived[half : half + 8] + arrived[half + 8 : half + 16]
+            if grad_part is not None:
+                grad_part = grad_part + arrived[half + 16 : half + 16 + half]
+        mean = jnp.transpose(jnp.broadcast_to(square[:1], (tokens, tokens)))[:half] / channels
         root = lax.rsqrt(mean + NORM_EPS)
         pre_act = partial * root[:, :rank]
         hidden = (pre_act * jax.nn.sigmoid(pre_act)).astype(jnp.bfloat16)
-        pre_acts[k] = pre_act
-        roots[k] = root
-        hiddens[k] = hidden
-        if not last:
-            streams[k + 1] = (wide + dot(hidden, weight_out(k), 1, 0)).astype(jnp.bfloat16)
+        pre_acts[k, rows] = pre_act
+        roots[k, rows] = root
+        hiddens[k, rows] = hidden
+        if k < sections - 1:
+            streams[k + 1, rows] = (
+                streams[k, rows].astype(jnp.float32) + dot(hidden, weight_out(k), 1, 0)
+            ).astype(jnp.bfloat16)
+        return grad_part
+
+    pass_on(0)
+    arrive(0)
+    states = [forward_send(0, h) for h in range(HALVES)]
+    for k in range(1, sections):
+        pass_on(k)
+        for h in range(HALVES):
+            forward_receive(k - 1, h, states[h])
+            if h == 0:
+                arrive(k)
+            states[h] = forward_send(k, h)
+    grad_partial = jnp.concatenate(
+        [forward_receive(sections - 1, h, states[h]) for h in range(HALVES)], axis=0
+    )
 
     def swap_part(unit):
         remote(
@@ -606,7 +641,7 @@
     square = jnp.zeros((8, 128), jnp.float32)
     grad = cotangent_ref[...].astype(jnp.float32)
     for k in reversed(range(sections)):
-        slot = 2 * sections - 1 - k
+        slot = sections - 1 - k
         pre_act = pre_acts[k]
         root = roots[k]
         squash = jax.nn.sigmoid(pre_act)
@@ -783,7 +818,9 @@
     piece_rows = in_rows + out_rows * tiles
 
     narrow, full = jnp.bfloat16, jnp.float32
-    slots = 2 * sections - 1
+    slots = sections - 1
+    chunks = HALVES * sections
+    half = tokens // HALVES
     units = 2 * sections
     dma = pltpu.SemaphoreType.DMA
     vmem = pl.BlockSpec(memory_space=pltpu.VMEM)
@@ -817,8 +854,10 @@
             pltpu.VMEM((sections, tokens, rank), full),
             pltpu.VMEM((sections, tokens, tokens), full),
             pltpu.VMEM((sections, tokens, rank), narrow),
-            pltpu.VMEM((slots, 2 * tokens + 16, rank), narrow),
-            pltpu.VMEM((slots, sections - 1, 2 * tokens + 16, rank), narrow),
+            pltpu.VMEM((slots, tokens, rank), narrow),
+            pltpu.VMEM((slots, sections - 1, tokens, rank), narrow),
+            pltpu.VMEM((chunks, 2 * half + 16, rank), narrow),
+            pltpu.VMEM((chunks, sections - 1, 2 * half + 16, rank), narrow),
             pltpu.VMEM((2, 8, 128), full),
             pltpu.VMEM((dp_count - 1, 8, 128), full),
             pltpu.VMEM((sections - 1, 8, 128), full),
@@ -833,6 +872,8 @@
             dma((sections, planes, CORES)),
             dma((slots, sections - 1)),
             dma((slots, sections - 1)),
+            dma((chunks, sections - 1)),
+            dma((chunks, sections - 1)),
             dma((units,)),
             dma((units,)),
             dma((units, planes - 1)),

time: 72.5 us -> 72 us (level)
  no operation moved by 1% of the time
where the time goes in v5:
time: 72 us; the launch traced here: 71.7 us
  Pallas kernels  71 us (99%)
    pallas_call x1, Pallas kernels, fast_shards(): pl.pallas_call(functools.partial(step_kernel, sections, planes), out_shap...  68.4 us
    pallas_call x1, Pallas kernels, fast_shards(): pl.pallas_call(adam_kernel, out_shape=(in_shape,) * 3 + (out_shape,) * 3,...  2.66 us

profile of v5, /device:TPU:0, one launch (start us, length us, event | category | flops | bytes accessed | tf_op | source)
XLA Modules:
  0.0 71.7 jit_solution(3743944548922672148)
XLA Ops:
  0.6 68.4 %shard_map.136 = (f32[448,128]{1,0:T(8,128)}, f32[16,3584]{1,0:T(8,128)}, f32[8,128]{1,0:T(8,128)}) custom-call(bf16[128,3584]{1,0:T(8,128)(2,1)} %bitcast.4, bf16[128,3584]{1,0:T(8,128)(2,1)} %bitcast.5, bf16[1,3584]{1,0:T(2,128)(2,1)} %gain_any.1, bf16[448,128]{1,0:T(8,128)(2,1)} %bitcast.6, bf16[16,3584]{1,0:T(8,128)(2,1)} %bitcast.7), custom_call_target="tpu_custom_call" | custom-call | tf_op jit(solution)/shard_map/pallas_call | solution.py:827
  69.0 2.7 %shard_map.137 = (f32[1,448,128]{2,1,0:T(8,128)}, f32[1,448,128]{2,1,0:T(8,128)}, f32[1,448,128]{2,1,0:T(8,128)}, f32[1,16,3584]{2,1,0:T(8,128)}, f32[1,16,3584]{2,1,0:T(8,128)}, /*index=5*/f32[1,16,3584]{2,1,0:T(8,128)}) custom-call(f32[8,128]{1,0:T(8,128)} %get-tuple-element.9.refs_0_, f32[448,128]{1,0:T(8,128)} %get-tuple-element.10.refs_1_, ...), custom_call_target="tpu_custom_call" | custom-call | tf_op jit(solution)/shard_map/pallas_call | solution.py:912

commit v6 on v5

--- a/solution.py
+++ b/solution.py
@@ -248,6 +248,7 @@
     from_core,
     chip_sums,
     from_planes,
+    relayed,
     totals,
     owned,
     streams,
@@ -278,6 +279,7 @@
     part_recv,
     sum_send,
     sum_recv,
+    relay_recv,
     total_send,
     total_recv,
     dp_send,
@@ -599,19 +601,62 @@
             parts[unit, :, core].astype(jnp.float32) + from_core[unit].astype(jnp.float32)
         ).astype(jnp.bfloat16)
         for offset in range(1, planes):
-            remote(
-                chip_sums.at[unit, lax.rem(plane + offset, planes)],
-                from_planes.at[unit, offset - 1],
-                sum_send.at[unit, offset - 1],
-                sum_recv.at[unit, offset - 1],
-                plane_peer(offset),
-            )
+            target = lax.rem(plane + offset, planes)
+            if unit == 0:
+                send_sum(unit, offset, target)
+                continue
+            ends = ((plane == 0) & (target == far)) | ((plane == far) & (target == 0))
+            later = ((plane == 1) & (target == far)) | ((plane == far - 1) & (target == 0))
+
+            @pl.when(jnp.logical_not(ends | later))
+            def _():
+                send_sum(unit, offset, target)
+
+            @pl.when(ends)
+            def _():
+                side = jnp.where(plane == 0, 0, 1)
+                relay = jnp.where(plane == 0, 1, far - 1)
+                send(
+                    chip_sums.at[unit, target],
+                    relayed.at[unit, side],
+                    sum_send.at[unit, offset - 1],
+                    relay_recv.at[unit, side],
+                    (me_s, relay * CORES + core),
+                )
+
+    def send_sum(unit, offset, target):
+        send(
+            chip_sums.at[unit, target],
+            from_planes.at[unit, offset - 1],
+            sum_send.at[unit, offset - 1],
+            sum_recv.at[unit, offset - 1],
+            (me_s, target * CORES + core),
+        )
+
+    def relay_sum(unit):
+        for side, relay, target in ((0, 1, far), (1, far - 1, 0)):
+
+            @pl.when(plane == relay)
+            def _():
+                landed(relayed.at[unit, side], relay_recv.at[unit, side])
+                chip_sums[unit, target] = (
+                    chip_sums[unit, target].astype(jnp.float32)
+                    + relayed[unit, side].astype(jnp.float32)
+                ).astype(jnp.bfloat16)
+                send_sum(unit, (target - relay) % planes, target)
 
     def send_total(unit):
         k, kind = unit // 2, unit % 2
         total = chip_sums[unit, plane].astype(jnp.float32)
         for offset in range(1, planes):
-            landed(from_planes.at[unit, offset - 1], sum_recv.at[unit, offset - 1])
+            source = lax.rem(plane + planes - offset, planes)
+            ends = ((plane == 0) & (source == far)) | ((plane == far) & (source == 0))
+            direct = jnp.logical_not(ends) if unit > 0 else plane >= 0
+
+            @pl.when(direct)
+            def _():
+                landed(from_planes.at[unit, offset - 1], sum_recv.at[unit, offset - 1])
+
             total = total + from_planes[unit, offset - 1].astype(jnp.float32)
         total = total.astype(jnp.bfloat16)
         totals[unit] = total
@@ -639,6 +684,16 @@
     for k in range(sections):
         landed(gain_of.at[k], gain_recv.at[k])
     square = jnp.zeros((8, 128), jnp.float32)
+    nothing = jnp.zeros((2 * sections - 1, in_rows, 128), jnp.bfloat16)
+
+    @pl.when(plane == 0)
+    def _():
+        from_planes[1:, 0] = nothing
+
+    @pl.when(plane == far)
+    def _():
+        from_planes[1:, far - 1] = nothing
+
     grad = cotangent_ref[...].astype(jnp.float32)
     for k in reversed(range(sections)):
         slot = sections - 1 - k
@@ -659,7 +714,10 @@
             grad_partial = dot(grad_rounded, weight_out(k - 1), 1, 1)
             sent[slot, :tokens] = grad_partial.astype(jnp.bfloat16)
             copies = swap(slot, tokens)
-        if k == sections - 1:
+        if k < sections - 1:
+            for unit in units_of(k + 1):
+                relay_sum(unit)
+        else:
             make_out_part(k, cotangent_ref[...])
         make_in_part(k, grad_act)
         if k > 0:
@@ -735,6 +793,9 @@
 
     for copy in started:
         copy.wait_send()
+    for unit in range(2 * sections):
+        for offset in range(1, planes):
+            landed(chip_sums.at[unit, 0], sum_send.at[unit, offset - 1])
     for k in range(sections):
         for offset in range(1, planes):
             target = lax.rem(plane + offset, planes)
@@ -848,6 +909,7 @@
             pltpu.VMEM((units, planes, in_rows, 128), narrow),
             pltpu.VMEM((units, planes, in_rows, 128), narrow),
             pltpu.VMEM((units, planes - 1, in_rows, 128), narrow),
+            pltpu.VMEM((units, 2, in_rows, 128), narrow),
             pltpu.VMEM((units, in_rows, 128), narrow),
             pltpu.VMEM((2, sections, in_rows, 128), narrow),
             pltpu.VMEM((sections, tokens, width), narrow),
@@ -878,6 +940,7 @@
             dma((units,)),
             dma((units, planes - 1)),
             dma((units, planes - 1)),
+            dma((units, 2)),
             dma((units,)),
             dma((2, sections)),
             dma((dp_count - 1,)),

time: 72 us -> 74.6 us (1.036)
  Pallas kernels: 71 us -> 73.7 us
    pallas_call x1, Pallas kernels: 68.4 us -> 71 us  [fast_shards(): pl.pallas_call(functools.partial(step_kernel, sections, planes), out_shap...]
where the time goes in v6:
time: 74.6 us; the launch traced here: 74.3 us
  Pallas kernels  73.7 us (99%)
    pallas_call x1, Pallas kernels, fast_shards(): pl.pallas_call(functools.partial(step_kernel, sections, planes), out_shap...  71 us
    pallas_call x1, Pallas kernels, fast_shards(): pl.pallas_call(adam_kernel, out_shape=(in_shape,) * 3 + (out_shape,) * 3,...  2.66 us

profile of v6, /device:TPU:0, one launch (start us, length us, event | category | flops | bytes accessed | tf_op | source)
XLA Modules:
  0.0 74.3 jit_solution(15165691273109578697)
XLA Ops:
  0.6 71.0 %shard_map.136 = (f32[448,128]{1,0:T(8,128)}, f32[16,3584]{1,0:T(8,128)}, f32[8,128]{1,0:T(8,128)}) custom-call(bf16[128,3584]{1,0:T(8,128)(2,1)} %bitcast.4, bf16[128,3584]{1,0:T(8,128)(2,1)} %bitcast.5, bf16[1,3584]{1,0:T(2,128)(2,1)} %gain_any.1, bf16[448,128]{1,0:T(8,128)(2,1)} %bitcast.6, bf16[16,3584]{1,0:T(8,128)(2,1)} %bitcast.7), custom_call_target="tpu_custom_call" | custom-call | tf_op jit(solution)/shard_map/pallas_call | solution.py:888
  71.6 2.7 %shard_map.137 = (f32[1,448,128]{2,1,0:T(8,128)}, f32[1,448,128]{2,1,0:T(8,128)}, f32[1,448,128]{2,1,0:T(8,128)}, f32[1,16,3584]{2,1,0:T(8,128)}, f32[1,16,3584]{2,1,0:T(8,128)}, /*index=5*/f32[1,16,3584]{2,1,0:T(8,128)}) custom-call(f32[8,128]{1,0:T(8,128)} %get-tuple-element.9.refs_0_, f32[448,128]{1,0:T(8,128)} %get-tuple-element.10.refs_1_, ...), custom_call_target="tpu_custom_call" | custom-call | tf_op jit(solution)/shard_map/pallas_call | solution.py:975

commit v7 on v5

--- a/solution.py
+++ b/solution.py
@@ -659,16 +659,21 @@
             grad_partial = dot(grad_rounded, weight_out(k - 1), 1, 1)
             sent[slot, :tokens] = grad_partial.astype(jnp.bfloat16)
             copies = swap(slot, tokens)
+        if 0 < k < sections - 1:
+            for unit in units_of(k + 1):
+                send_chip_sums(unit)
         if k == sections - 1:
             make_out_part(k, cotangent_ref[...])
         make_in_part(k, grad_act)
         if k > 0:
             make_out_part(k - 1, grad_rounded)
-        if k == 0 and sections > 2:
-            for unit in units_of(k + 2):
-                square = square + send_total(unit)
-        for unit in units_of(k):
-            send_chip_sums(unit)
+        else:
+            for unit in units_of(1):
+                send_chip_sums(unit)
+            if sections > 2:
+                for unit in units_of(2):
+                    square = square + send_total(unit)
+            send_chip_sums(0)
         if 0 < k < sections - 2:
             for unit in units_of(k + 2):
                 square = square + send_total(unit)

time: 72 us -> 73 us (1.014)
  Pallas kernels: 71 us -> 72.1 us
    pallas_call x1, Pallas kernels: 68.4 us -> 69.5 us  [fast_shards(): pl.pallas_call(functools.partial(step_kernel, sections, planes), out_shap...]
where the time goes in v7:
time: 73 us; the launch traced here: 72.8 us
  Pallas kernels  72.1 us (99%)
    pallas_call x1, Pallas kernels, fast_shards(): pl.pallas_call(functools.partial(step_kernel, sections, planes), out_shap...  69.5 us
    pallas_call x1, Pallas kernels, fast_shards(): pl.pallas_call(adam_kernel, out_shape=(in_shape,) * 3 + (out_shape,) * 3,...  2.66 us

profile of v7, /device:TPU:0, one launch (start us, length us, event | category | flops | bytes accessed | tf_op | source)
XLA Modules:
  0.0 72.8 jit_solution(9158150797188243179)
XLA Ops:
  0.6 69.5 %shard_map.136 = (f32[448,128]{1,0:T(8,128)}, f32[16,3584]{1,0:T(8,128)}, f32[8,128]{1,0:T(8,128)}) custom-call(bf16[128,3584]{1,0:T(8,128)(2,1)} %bitcast.4, bf16[128,3584]{1,0:T(8,128)(2,1)} %bitcast.5, bf16[1,3584]{1,0:T(2,128)(2,1)} %gain_any.1, bf16[448,128]{1,0:T(8,128)(2,1)} %bitcast.6, bf16[16,3584]{1,0:T(8,128)(2,1)} %bitcast.7), custom_call_target="tpu_custom_call" | custom-call | tf_op jit(solution)/shard_map/pallas_call | solution.py:832
  70.1 2.7 %shard_map.137 = (f32[1,448,128]{2,1,0:T(8,128)}, f32[1,448,128]{2,1,0:T(8,128)}, f32[1,448,128]{2,1,0:T(8,128)}, f32[1,16,3584]{2,1,0:T(8,128)}, f32[1,16,3584]{2,1,0:T(8,128)}, /*index=5*/f32[1,16,3584]{2,1,0:T(8,128)}) custom-call(f32[8,128]{1,0:T(8,128)} %get-tuple-element.9.refs_0_, f32[448,128]{1,0:T(8,128)} %get-tuple-element.10.refs_1_, ...), custom_call_target="tpu_custom_call" | custom-call | tf_op jit(solution)/shard_map/pallas_call | solution.py:917
